TPU v7x, 512 devices: a whole 4x4x16 slice. The times are simulated.
512 devices in a mesh: seq: 32 (over y, z_lo), dp: 16 (over z_hi, x, core).
Axes of the slice: x: 4, y: 4, z: 16 (z_hi: 2, z_lo: 8; z = z_hi * 8 + z_lo), core: 2. Of those that a mesh axis runs over, the one named last changes fastest.
Arguments:
- tokens: bfloat16 [16, 8192, 768], P('dp', 'seq'), may hold values from -6 to 6
- cotangent: bfloat16 [16, 8192, 768], P('dp', 'seq'), may hold values from -6 to 6
- conv_kernel: float32 [3, 3, 768], replicated, may hold values from -3 to 3
- point_weight: bfloat16 [3, 768, 768], replicated, may hold values from -0.21875 to 0.21875
Outputs:
- grad_tokens: bfloat16 [16, 8192, 768], P('dp', 'seq')
- grad_point: float32 [3, 768, 768], P(None, 'seq', 'dp')
- grad_kernel: float32 [3, 3, 768], replicated
All inputs are finite; a program needn't handle non-finite values.
Results may differ from a plain program's by a relative error of at most 0.035.
Values may be sent and summed in bfloat16 or wider, within the bound.
A program may use at most 64 MiB of HBM per device.

v0:
```python
import math

import jax
import jax.numpy as jnp
from jax import lax
from jax.sharding import PartitionSpec as P

STRIDE0 = 4


EPSILON = 1e-06


def shifted(block, axis, distance):
    devices = range(lax.axis_size(axis))
    route = [(i - distance, i) for i in devices if i - distance in devices]
    return lax.ppermute(block, axis, route)


def tap_pieces(values, distance):
    from_below = shifted(values, "seq", distance)
    from_above = shifted(values, "seq", -distance)
    return (from_below, from_above)


def grad_pieces(values, distance):
    from_below = shifted(values, "seq", distance)
    from_above = shifted(values, "seq", -distance)
    return (from_below, from_above)


def gelu_back(hidden, spread):
    return jax.vjp(jax.nn.gelu, hidden)[1](spread)[0]


def local(tokens, cotangent, conv_kernel, point_weight):
    stream = tokens[0]
    row_count = stream.shape[0]
    layer_count = conv_kernel.shape[0]
    stored = []
    for layer_index in range(layer_count):
        distance = STRIDE0 * 2**layer_index
        stream_wide = stream.astype(jnp.float32)
        inv_rms = lax.rsqrt(jnp.mean(stream_wide * stream_wide, axis=-1, keepdims=True) + EPSILON)
        normal = stream_wide * inv_rms
        normed_bf = normal.astype(jnp.bfloat16)
        from_below, from_above = tap_pieces(normed_bf, distance)
        kernel_row = conv_kernel[layer_index]
        hidden = (
            kernel_row[0] * from_below.astype(jnp.float32)
            + kernel_row[1] * normed_bf.astype(jnp.float32)
            + kernel_row[2] * from_above.astype(jnp.float32)
        )
        active = jax.nn.gelu(hidden).astype(jnp.bfloat16)
        stream = (
            stream_wide
            + jnp.dot(active, point_weight[layer_index], preferred_element_type=jnp.float32)
        ).astype(jnp.bfloat16)
        stored.append((inv_rms, normal, normed_bf, from_below, from_above, hidden, active))
    gradient = cotangent[0].astype(jnp.float32)
    point_parts = [None] * layer_count
    kernel_parts = [None] * layer_count
    for layer_index in reversed(range(layer_count)):
        distance = STRIDE0 * 2**layer_index
        inv_rms, normal, normed_bf, from_below, from_above, hidden, active = stored[layer_index]
        kernel_row = conv_kernel[layer_index]
        upstream = gradient.astype(jnp.bfloat16)
        partial_wide = jnp.einsum("tc,td->cd", active, upstream, preferred_element_type=jnp.float32)
        partial_value = lax.optimization_barrier(partial_wide.astype(jnp.bfloat16)).astype(
            jnp.float32
        )
        spread = jnp.einsum(
            "td,cd->tc", upstream, point_weight[layer_index], preferred_element_type=jnp.float32
        )
        grad_hidden = gelu_back(hidden, spread).astype(jnp.bfloat16)
        grad_wide = grad_hidden.astype(jnp.float32)
        kernel_term = jnp.stack(
            [
                jnp.sum(grad_wide * from_below.astype(jnp.float32), axis=0),
                jnp.sum(grad_wide * normed_bf.astype(jnp.float32), axis=0),
                jnp.sum(grad_wide * from_above.astype(jnp.float32), axis=0),
            ]
        )
        grad_from_below, grad_from_above = grad_pieces(grad_hidden, distance)
        grad_normed = (
            kernel_row[1] * grad_wide
            + kernel_row[0] * grad_from_above.astype(jnp.float32)
            + kernel_row[2] * grad_from_below.astype(jnp.float32)
        )
        gradient = gradient + inv_rms * (
            grad_normed - normal * jnp.mean(grad_normed * normal, axis=-1, keepdims=True)
        )
        point_parts[layer_index] = partial_value
        kernel_parts[layer_index] = kernel_term
    point_stack = jnp.stack(point_parts)
    kernel_stack = jnp.stack(kernel_parts)
    stacked_seq = lax.psum_scatter(
        point_stack.astype(jnp.bfloat16), "seq", scatter_dimension=1, tiled=True
    )
    point_stack = lax.psum_scatter(stacked_seq, "dp", scatter_dimension=2, tiled=True).astype(
        jnp.float32
    )
    kernel_stack = lax.psum(kernel_stack, ("seq", "dp"))
    factor = 1.0 / math.sqrt(lax.axis_size("dp") * lax.axis_size("seq") * row_count)
    return (gradient.astype(jnp.bfloat16)[None], point_stack * factor, kernel_stack * factor)


def solution(mesh):
    return jax.shard_map(
        local,
        mesh=mesh,
        in_specs=(P("dp", "seq", None), P("dp", "seq", None), P(), P()),
        out_specs=(P("dp", "seq", None), P(None, "seq", "dp"), P()),
        check_vma=False,
    )
```

profile of v0, /device:TPU:1, one launch (start us, length us, event | category | flops | bytes accessed | tf_op | source)
XLA Modules:
  0.0 518.4 jit_solution(2324350149380428801)
XLA Ops:
  7.2 1.2 fusion.52
  8.4 1.1 fusion.15
  9.6 1.3 collective-permute-start.1
  10.9 10.3 %collective-permute-start = (bf16[256,768]{1,0:T(8,128)(2,1)S(1)}, bf16[256,768]{1,0:T(8,128)(2,1)S(1)}, u32[]{:S(2)}, u32[]{:S(2)}) collective-permute-start(bf16[256,768]{1,0:T(8,128)(2,1)S(1)} %fusion.15), channel_id=1, source_target_pairs={{0,64},{16,80},{32,96},{48,112},{64,128},{80,144},{96,160},{112,17... | collective-permute-start | bytes 1179656 | tf_op jit(solution)/shard_map/ppermute | solution.py:17
  22.1 55.8 %collective-permute-done.1 = bf16[256,768]{1,0:T(8,128)(2,1)S(1)} collective-permute-done((bf16[256,768]{1,0:T(8,128)(2,1)S(1)}, bf16[256,768]{1,0:T(8,128)(2,1)S(1)}, u32[]{:S(2)}, u32[]{:S(2)}) %collective-permute-start.1) | collective-permute-done | bytes 393248 | tf_op jit(solution)/shard_map/ppermute | solution.py:17
  77.9 1.5 multiply_convert_fusion.2
  79.5 2.0 multiply_reduce_fusion.3
  81.6 1.3 collective-permute-start.3
  82.9 12.2 %collective-permute-start.2 = (bf16[256,768]{1,0:T(8,128)(2,1)S(1)}, bf16[256,768]{1,0:T(8,128)(2,1)S(1)}, u32[]{:S(2)}, u32[]{:S(2)}) collective-permute-start(bf16[256,768]{1,0:T(8,128)(2,1)S(1)} %multiply_convert_fusion.4), channel_id=1, source_target_pairs={{0,128},{16,144},{32,160},{48,176},{64,192},{80,208},{96,224},{112... | collective-permute-start | bytes 1179656 | tf_op jit(solution)/shard_map/ppermute | solution.py:17
  95.1 5.6 %collective-permute-done.3 = bf16[256,768]{1,0:T(8,128)(2,1)S(1)} collective-permute-done((bf16[256,768]{1,0:T(8,128)(2,1)S(1)}, bf16[256,768]{1,0:T(8,128)(2,1)S(1)}, u32[]{:S(2)}, u32[]{:S(2)}) %collective-permute-start.3) | collective-permute-done | bytes 393248 | tf_op jit(solution)/shard_map/ppermute | solution.py:17
  102.8 1.3 collective-permute-start.5
  104.1 6.7 %collective-permute-start.4 = (bf16[256,768]{1,0:T(8,128)(2,1)S(1)}, bf16[256,768]{1,0:T(8,128)(2,1)S(1)}, u32[]{:S(2)}, u32[]{:S(2)}) collective-permute-start(bf16[256,768]{1,0:T(8,128)(2,1)S(1)} %multiply_convert_fusion.3), channel_id=1, source_target_pairs={{0,256},{16,272},{32,288},{48,304},{64,320},{80,336},{96,352},{112... | collective-permute-start | bytes 1179656 | tf_op jit(solution)/shard_map/ppermute | solution.py:17
  110.8 4.8 collective-permute-done.5
  117.5 5.6 %collective-permute-start.7 = (bf16[256,768]{1,0:T(8,128)(2,1)S(1)}, bf16[256,768]{1,0:T(8,128)(2,1)S(1)}, u32[]{:S(2)}, u32[]{:S(2)}) collective-permute-start(bf16[256,768]{1,0:T(8,128)(2,1)S(1)} %fusion.51), channel_id=1, source_target_pairs={{0,256},{16,272},{32,288},{48,304},{64,320},{80,336},{96,352},{112... | collective-permute-start | bytes 1179656 | tf_op jit(solution)/shard_map/ppermute | solution.py:17
  123.2 1.3 collective-permute-start.6
  124.5 3.4 collective-permute-done.7
  127.8 5.3 %collective-permute-done.6 = bf16[256,768]{1,0:T(8,128)(2,1)S(1)} collective-permute-done((bf16[256,768]{1,0:T(8,128)(2,1)S(1)}, bf16[256,768]{1,0:T(8,128)(2,1)S(1)}, u32[]{:S(2)}, u32[]{:S(2)}) %collective-permute-start.6) | collective-permute-done | bytes 393248 | tf_op jit(solution)/shard_map/ppermute | solution.py:17
  135.2 2.5 collective-permute-start.9
  137.7 1.5 collective-permute-start.8
  140.6 1.8 collective-permute-done.9
  142.4 3.8 collective-permute-done.8
  148.2 3.0 copy.7
  151.3 2.5 copy.12
  153.9 2.3 fusion.37
  156.2 2.5 collective-permute-start.11
  158.6 1.3 collective-permute-start.10
  160.0 3.3 collective-permute-done.11
  163.3 77.1 %collective-permute-done.10 = bf16[256,768]{1,0:T(8,128)(2,1)S(1)} collective-permute-done((bf16[256,768]{1,0:T(8,128)(2,1)S(1)}, bf16[256,768]{1,0:T(8,128)(2,1)S(1)}, u32[]{:S(2)}, u32[]{:S(2)}) %collective-permute-start.10) | collective-permute-done | bytes 393248 | tf_op jit(solution)/shard_map/ppermute | solution.py:17
  241.2 106.1 %psum.7 = f32[3,3,768]{2,1,0:T(4,128)S(1)} all-reduce(f32[3,3,768]{2,1,0:T(4,128)S(1)} %pad_maximum_fusion.1), channel_id=1, replica_groups=mesh['seq'=32,'dp'=16] {'seq','dp'}, use_global_device_ids=true, to_apply=%region_17.0 | all-reduce | flops 6912 | bytes 55296 | tf_op jit(solution)/shard_map/psum | solution.py:103
  347.2 1.2 fusion.74
  348.4 42.0 %reduce-scatter.7.cloned.1.call-done = bf16[24,2304]{1,0:T(8,128)(2,1)} async-done(((bf16[768,2304]{1,0:T(8,128)(2,1)}), bf16[24,2304]{1,0:T(8,128)(2,1)}) %reduce-scatter.7.cloned.1.call-update) | async-done | bytes 110608
  393.6 116.4 %reduce-scatter.9.cloned.1.call-done = bf16[48,72]{1,0:T(8,128)(2,1)} async-done(((bf16[768,72]{1,0:T(8,128)(2,1)}), bf16[48,72]{1,0:T(8,128)(2,1)}) %reduce-scatter.9.cloned.1.call-update) | async-done | bytes 6928
  (54 shorter events, 16.0 us)
Async XLA Ops:
  7.2 72.3 %copy-start = (bf16[1,256,768]{2,1,0:T(8,128)(2,1)S(1)}, bf16[1,256,768]{2,1,0:T(8,128)(2,1)}, u32[]{:S(2)}) copy-start(bf16[1,256,768]{2,1,0:T(8,128)(2,1)} %param.4) | copy-start | bytes 1179652
  7.2 383.2 %reduce-scatter.7.cloned.1.call-start = ((), (), s32[]{:S(2)}) async-start(), calls=%async_computation.2 | async-start | bytes 3649536
  9.6 68.4 %collective-permute-start.1 = (bf16[256,768]{1,0:T(8,128)(2,1)S(1)}, bf16[256,768]{1,0:T(8,128)(2,1)S(1)}, u32[]{:S(2)}, u32[]{:S(2)}) collective-permute-start(bf16[256,768]{1,0:T(8,128)(2,1)S(1)} %fusion.15), channel_id=1, source_target_pairs={{64,0},{80,16},{96,32},{112,48},{128,64},{144,80},{160,96},{176,11... | collective-permute-start | bytes 1179656 | tf_op jit(solution)/shard_map/ppermute | solution.py:17
  10.9 67.1 %collective-permute-start = (bf16[256,768]{1,0:T(8,128)(2,1)S(1)}, bf16[256,768]{1,0:T(8,128)(2,1)S(1)}, u32[]{:S(2)}, u32[]{:S(2)}) collective-permute-start(bf16[256,768]{1,0:T(8,128)(2,1)S(1)} %fusion.15), channel_id=1, source_target_pairs={{0,64},{16,80},{32,96},{48,112},{64,128},{80,144},{96,160},{112,17... | collective-permute-start | bytes 1179656 | tf_op jit(solution)/shard_map/ppermute | solution.py:17
  79.5 22.6 %copy-start.1 = (bf16[3,768,768]{2,1,0:T(8,128)(2,1)S(1)}, bf16[3,768,768]{2,1,0:T(8,128)(2,1)}, u32[]{:S(2)}) copy-start(bf16[3,768,768]{2,1,0:T(8,128)(2,1)} %param.7) | copy-start | bytes 10616836
  81.6 19.0 %collective-permute-start.3 = (bf16[256,768]{1,0:T(8,128)(2,1)S(1)}, bf16[256,768]{1,0:T(8,128)(2,1)S(1)}, u32[]{:S(2)}, u32[]{:S(2)}) collective-permute-start(bf16[256,768]{1,0:T(8,128)(2,1)S(1)} %multiply_convert_fusion.4), channel_id=1, source_target_pairs={{128,0},{144,16},{160,32},{176,48},{192,64},{208,80},{224,96},{240... | collective-permute-start | bytes 1179656 | tf_op jit(solution)/shard_map/ppermute | solution.py:17
  82.9 18.6 %collective-permute-start.2 = (bf16[256,768]{1,0:T(8,128)(2,1)S(1)}, bf16[256,768]{1,0:T(8,128)(2,1)S(1)}, u32[]{:S(2)}, u32[]{:S(2)}) collective-permute-start(bf16[256,768]{1,0:T(8,128)(2,1)S(1)} %multiply_convert_fusion.4), channel_id=1, source_target_pairs={{0,128},{16,144},{32,160},{48,176},{64,192},{80,208},{96,224},{112... | collective-permute-start | bytes 1179656 | tf_op jit(solution)/shard_map/ppermute | solution.py:17
  102.1 14.5 %copy-start.2 = (bf16[1,256,768]{2,1,0:T(8,128)(2,1)S(1)}, bf16[1,256,768]{2,1,0:T(8,128)(2,1)}, u32[]{:S(2)}) copy-start(bf16[1,256,768]{2,1,0:T(8,128)(2,1)} %param.5) | copy-start | bytes 1179652
  102.8 12.8 %collective-permute-start.5 = (bf16[256,768]{1,0:T(8,128)(2,1)S(1)}, bf16[256,768]{1,0:T(8,128)(2,1)S(1)}, u32[]{:S(2)}, u32[]{:S(2)}) collective-permute-start(bf16[256,768]{1,0:T(8,128)(2,1)S(1)} %multiply_convert_fusion.3), channel_id=1, source_target_pairs={{256,0},{272,16},{288,32},{304,48},{320,64},{336,80},{352,96},{368... | collective-permute-start | bytes 1179656 | tf_op jit(solution)/shard_map/ppermute | solution.py:17
  104.1 12.5 %collective-permute-start.4 = (bf16[256,768]{1,0:T(8,128)(2,1)S(1)}, bf16[256,768]{1,0:T(8,128)(2,1)S(1)}, u32[]{:S(2)}, u32[]{:S(2)}) collective-permute-start(bf16[256,768]{1,0:T(8,128)(2,1)S(1)} %multiply_convert_fusion.3), channel_id=1, source_target_pairs={{0,256},{16,272},{32,288},{48,304},{64,320},{80,336},{96,352},{112... | collective-permute-start | bytes 1179656 | tf_op jit(solution)/shard_map/ppermute | solution.py:17
  117.5 10.3 %collective-permute-start.7 = (bf16[256,768]{1,0:T(8,128)(2,1)S(1)}, bf16[256,768]{1,0:T(8,128)(2,1)S(1)}, u32[]{:S(2)}, u32[]{:S(2)}) collective-permute-start(bf16[256,768]{1,0:T(8,128)(2,1)S(1)} %fusion.51), channel_id=1, source_target_pairs={{0,256},{16,272},{32,288},{48,304},{64,320},{80,336},{96,352},{112... | collective-permute-start | bytes 1179656 | tf_op jit(solution)/shard_map/ppermute | solution.py:17
  123.2 10.0 %collective-permute-start.6 = (bf16[256,768]{1,0:T(8,128)(2,1)S(1)}, bf16[256,768]{1,0:T(8,128)(2,1)S(1)}, u32[]{:S(2)}, u32[]{:S(2)}) collective-permute-start(bf16[256,768]{1,0:T(8,128)(2,1)S(1)} %fusion.51), channel_id=1, source_target_pairs={{256,0},{272,16},{288,32},{304,48},{320,64},{336,80},{352,96},{368... | collective-permute-start | bytes 1179656 | tf_op jit(solution)/shard_map/ppermute | solution.py:17
  135.2 7.2 %collective-permute-start.9 = (bf16[256,768]{1,0:T(8,128)(2,1)S(1)}, bf16[256,768]{1,0:T(8,128)(2,1)S(1)}, u32[]{:S(2)}, u32[]{:S(2)}) collective-permute-start(bf16[256,768]{1,0:T(8,128)(2,1)S(1)} %fusion.44), channel_id=1, source_target_pairs={{0,128},{16,144},{32,160},{48,176},{64,192},{80,208},{96,224},{112... | collective-permute-start | bytes 1179656 | tf_op jit(solution)/shard_map/ppermute | solution.py:17
  137.7 8.5 %collective-permute-start.8 = (bf16[256,768]{1,0:T(8,128)(2,1)S(1)}, bf16[256,768]{1,0:T(8,128)(2,1)S(1)}, u32[]{:S(2)}, u32[]{:S(2)}) collective-permute-start(bf16[256,768]{1,0:T(8,128)(2,1)S(1)} %fusion.44), channel_id=1, source_target_pairs={{128,0},{144,16},{160,32},{176,48},{192,64},{208,80},{224,96},{240... | collective-permute-start | bytes 1179656 | tf_op jit(solution)/shard_map/ppermute | solution.py:17
  153.8 356.2 %reduce-scatter.9.cloned.1.call-start = ((), (), s32[]{:S(2)}) async-start(), calls=%async_computation.3 | async-start | bytes 208896
  156.2 7.1 %collective-permute-start.11 = (bf16[256,768]{1,0:T(8,128)(2,1)S(1)}, bf16[256,768]{1,0:T(8,128)(2,1)S(1)}, u32[]{:S(2)}, u32[]{:S(2)}) collective-permute-start(bf16[256,768]{1,0:T(8,128)(2,1)S(1)} %fusion.37), channel_id=1, source_target_pairs={{0,64},{16,80},{32,96},{48,112},{64,128},{80,144},{96,160},{112,17... | collective-permute-start | bytes 1179656 | tf_op jit(solution)/shard_map/ppermute | solution.py:17
  158.6 81.8 %collective-permute-start.10 = (bf16[256,768]{1,0:T(8,128)(2,1)S(1)}, bf16[256,768]{1,0:T(8,128)(2,1)S(1)}, u32[]{:S(2)}, u32[]{:S(2)}) collective-permute-start(bf16[256,768]{1,0:T(8,128)(2,1)S(1)} %fusion.37), channel_id=1, source_target_pairs={{64,0},{80,16},{96,32},{112,48},{128,64},{144,80},{160,96},{176,11... | collective-permute-start | bytes 1179656 | tf_op jit(solution)/shard_map/ppermute | solution.py:17
Sparse Core Ops, SparseCore 0:
  154.0 236.4 reduce-scatter.6
  395.7 114.2 reduce-scatter.8
where the time goes:
time: 520 us; the launch traced here: 518 us
  waiting for transfers between devices  321 us (62%)
  blocking collectives  106 us (20%)
  starting transfers between devices  47.7 us (9%)
  between operations  14.4 us (3%)
  other arithmetic  10.2 us (2%)
  local copies, waits for them, and re-layouts  10 us (2%)
  matrix products  8.74 us (2%)
    ppermute x12, waiting for transfers between devices, shifted(): return lax.ppermute(block, axis, route)  163 us
    unnamed x4, waiting for transfers between devices  158 us
    psum x1, blocking collectives, local(): kernel_stack = lax.psum(kernel_stack, ('seq', 'dp'))  106 us
    ppermute x12, starting transfers between devices, shifted(): return lax.ppermute(block, axis, route)  47.7 us
  transfers between devices with their start and end apart: 14, of which 13 were waited for; matrix products, arithmetic and copies ran while one was open for 1% of the time, Pallas kernels for 0%

commit v1 on v0

v1 whole, which is shorter than its diff:
```python
import functools
import math

import jax
import jax.numpy as jnp
from jax import lax
from jax.experimental import pallas as pl
from jax.experimental.pallas import tpu as pltpu

EPSILON = 1e-06
MESH = pl.DeviceIdType.MESH
F32 = jnp.float32
BF16 = jnp.bfloat16

C = 768
LAYERS = 3
CHAIN = 8
ROWS = 16
PARTS = 2
SLAB = 256
COLS = 256
GELU_A = math.sqrt(2.0 / math.pi)
GELU_B = 0.044715


def kernel(factor, tok, cot, taps, weight, out, out_point, out_taps, *scratch):
    (xin, normed, normal, inverse, slope, active, up, grad, grad_hid, ready, w, acc, terms, sibling, summed, from_x, turned,
     to_y, from_y, to_z, from_z, to_block, from_block, taps_acc, taps_out, taps_in,
     tok_send, tok_recv, cot_send, cot_recv, out_send, out_recv, own_sem, w_sem, red_send, red_recv) = scratch
    seq = lax.axis_index("seq")
    dp = lax.axis_index("dp")
    k, c = seq // 4, seq % 4
    y, h = seq // 8, (seq // 4) % 2
    zh, x, core = dp // 8, (dp // 2) % 4, dp % 2
    block = zh * 2 + h

    def chain_peer(i):
        j = (k + i) % CHAIN
        return j, (j * 4 + c, dp)

    def step_peer(stage, i):
        if stage == 0:
            return 1 - core, (seq, dp + 1 - 2 * core)
        if stage == 1:
            place = (x + i) % 4
            return place, (seq, zh * 8 + place * 2 + core)
        if stage == 2:
            place = (y + i) % 4
            return place, (place * 8 + h * 4 + c, dp)
        if stage == 3:
            place = (c + i) % 4
            return place, (seq - c + place, dp)
        place = (block + i) % 4
        return place, (y * 8 + (place % 2) * 4 + c, (place // 2) * 8 + dp % 8)

    barrier = pltpu.get_barrier_semaphore()

    def greet(peer):
        pl.semaphore_signal(barrier, inc=1, device_id=peer, device_id_type=MESH)

    @pl.loop(1, CHAIN)
    def _(i):
        greet(chain_peer(i)[1])

    greet(step_peer(0, 1)[1])

    @pl.loop(1, 4)
    def _(i):
        greet(step_peer(1, i)[1])
        greet(step_peer(3, i)[1])

    @pl.loop(0, 2)
    def _(i):
        greet((y * 8 + i * 4 + c, (1 - zh) * 8 + dp % 8))

    pl.semaphore_wait(barrier, 16)

    def rows_of(j, a):
        return pl.ds(pl.multiple_of(j * (PARTS * ROWS) + a * ROWS, ROWS), ROWS)

    def crossing_first(t):
        return 2 * t + 1 - 7 * (t // 4)

    def deal(src, dst_of, send, recv, a, i):
        j, peer = chain_peer(i)
        return pltpu.make_async_remote_copy(
            src_ref=src.at[rows_of(j, a)], dst_ref=dst_of(a, k), send_sem=send.at[a, i - 1], recv_sem=recv.at[a, i - 1],
            device_id=peer, device_id_type=MESH)

    def dealt(src, dst_of, send, recv, a, i):
        j = (k + CHAIN - i) % CHAIN
        return pltpu.make_async_remote_copy(
            src_ref=src.at[rows_of(j, a)], dst_ref=dst_of(a, j), send_sem=send.at[a, i - 1], recv_sem=recv.at[a, i - 1],
            device_id=chain_peer(i)[1], device_id_type=MESH)

    def tok_slot(a, j):
        return xin.at[a, j]

    def cot_slot(a, j):
        return up.at[LAYERS - 1, a, j]

    def own_tok(a):
        return pltpu.make_async_copy(tok.at[rows_of(k, a)], xin.at[a, k], own_sem.at[a])

    def own_cot(a):
        return pltpu.make_async_copy(cot.at[rows_of(k, a)], up.at[LAYERS - 1, a, k], own_sem.at[PARTS + a])

    def own_out(a):
        return pltpu.make_async_copy(ready.at[a, k], out.at[rows_of(k, a)], own_sem.at[2 * PARTS + a])

    def give_back(a, i):
        j, peer = chain_peer(i)
        return pltpu.make_async_remote_copy(
            src_ref=ready.at[a, j], dst_ref=out.at[rows_of(k, a)], send_sem=out_send.at[a, i - 1],
            recv_sem=out_recv.at[a, i - 1], device_id=peer, device_id_type=MESH)

    def given_back(a, i):
        j = (k + CHAIN - i) % CHAIN
        return pltpu.make_async_remote_copy(
            src_ref=ready.at[a, j], dst_ref=out.at[rows_of(j, a)], send_sem=out_send.at[a, i - 1],
            recv_sem=out_recv.at[a, i - 1], device_id=chain_peer(i)[1], device_id_type=MESH)

    for a in range(PARTS):
        @pl.loop(0, CHAIN - 1)
        def _(t):
            deal(tok, tok_slot, tok_send, tok_recv, a, crossing_first(t)).start()

        own_tok(a).start()
    for a in range(PARTS):
        @pl.loop(0, CHAIN - 1)
        def _(t):
            deal(cot, cot_slot, cot_send, cot_recv, a, crossing_first(t)).start()

        own_cot(a).start()
    for layer in range(LAYERS):
        pltpu.make_async_copy(weight.at[layer], w.at[layer], w_sem.at[layer]).start()

    zeros = jnp.zeros((4, ROWS, C), BF16)
    for layer in range(LAYERS):
        for a in range(PARTS):
            normed[layer, a, 0:4] = zeros
            normed[layer, a, 12:16] = zeros
    grad_hid[0:4] = zeros
    grad_hid[12:16] = zeros
    taps_acc[...] = jnp.zeros_like(taps_acc)
    taps_out[...] = jnp.zeros_like(taps_out)

    def forward(a):
        for layer in range(LAYERS):
            shift = 2**layer

            @pl.loop(0, CHAIN)
            def _(j):
                value = xin[a, j].astype(F32)
                mean = jnp.sum(value * value, axis=-1, keepdims=True) * (1.0 / C)
                inv = lax.rsqrt(mean + EPSILON)
                value = value * inv
                inverse[layer, a, j] = jnp.broadcast_to(inv, (ROWS, 128))
                normal[layer, a, j] = value
                normed[layer, a, 4 + j] = value.astype(BF16)

            @pl.loop(0, CHAIN)
            def _(j):
                hid = (
                    taps[layer, 0:1, :] * normed[layer, a, 4 + j - shift].astype(F32)
                    + taps[layer, 1:2, :] * normed[layer, a, 4 + j].astype(F32)
                    + taps[layer, 2:3, :] * normed[layer, a, 4 + j + shift].astype(F32)
                )
                square = hid * hid
                tanh = jnp.tanh(GELU_A * hid * (1.0 + GELU_B * square))
                half = 0.5 * (1.0 + tanh)
                active[layer, a, j] = (hid * half).astype(BF16)
                slope[layer, a, j] = half + (0.5 * GELU_A) * hid * (1.0 - tanh * tanh) * (1.0 + (3.0 * GELU_B) * square)

            if layer == LAYERS - 1:
                continue
            if a == 0:
                pltpu.make_async_copy(weight.at[layer], w.at[layer], w_sem.at[layer]).wait()
            for n in range(C // COLS):
                cols = slice(n * COLS, (n + 1) * COLS)
                product = jnp.dot(active[layer, a].reshape(CHAIN * ROWS, C), w[layer, :, cols], preferred_element_type=F32)
                xin[a, :, :, cols] = (
                    xin[a, :, :, cols].astype(F32) + product.reshape(CHAIN, ROWS, COLS)).astype(BF16)

    def backward(a, layer):
        shift = 2**layer
        if a == 0 and layer == LAYERS - 1:
            pltpu.make_async_copy(weight.at[layer], w.at[layer], w_sem.at[layer]).wait()
        for n in range(C // COLS):
            cols = slice(n * COLS, (n + 1) * COLS)
            spread = lax.dot_general(
                up[layer, a].reshape(CHAIN * ROWS, C), w[layer, cols, :], (((1,), (1,)), ((), ())),
                preferred_element_type=F32)
            grad_hid[4:12, :, cols] = (spread.reshape(CHAIN, ROWS, COLS) * slope[layer, a, :, :, cols]).astype(BF16)

        @pl.loop(0, CHAIN)
        def _(j):
            mid = grad_hid[4 + j].astype(F32)
            for t in range(3):
                term = mid * normed[layer, a, 4 + j + (t - 1) * shift].astype(F32)
                taps_acc[layer, t] += term[0:8] + term[8:16]
            moved = (
                taps[layer, 1:2, :] * mid
                + taps[layer, 0:1, :] * grad_hid[4 + j + shift].astype(F32)
                + taps[layer, 2:3, :] * grad_hid[4 + j - shift].astype(F32)
            )
            value = normal[layer, a, j]
            mean = jnp.sum(moved * value, axis=-1, keepdims=True) * (1.0 / C)
            before = up[layer, a, j].astype(F32) if layer == LAYERS - 1 else grad[j]
            after = before + inverse[layer, a, j, :, 0:1] * (moved - value * mean)
            if layer > 0:
                grad[j] = after
                up[layer - 1, a, j] = after.astype(BF16)
            else:
                ready[a, j] = after.astype(BF16)

    def parcel(layer, stage, i, mine):
        place, peer = step_peer(stage, i)
        if stage == 0:
            src, dst = terms.at[layer, place], sibling.at[layer]
        elif stage == 1:
            src, dst = summed.at[layer, :, place], from_x.at[layer, i - 1]
        elif stage == 2:
            src, dst = to_y.at[layer, place], from_y.at[layer, i - 1]
        elif stage == 3:
            src, dst = to_z.at[layer, place], from_z.at[layer, i - 1]
        else:
            src, dst = to_block.at[layer, place % 2], from_block.at[layer, i - 1]
        if mine:
            src, dst = taps_out.at[layer, stage], taps_in.at[layer, stage, i - 1]
        kind = 1 if mine else 0
        return pltpu.make_async_remote_copy(
            src_ref=src, dst_ref=dst, send_sem=red_send.at[layer, stage, i - 1, kind],
            recv_sem=red_recv.at[layer, stage, i - 1, kind], device_id=peer, device_id_type=MESH)

    def partners(stage):
        return range(1, 2 if stage == 0 else 4)

    def send(layer, stage):
        for i in partners(stage):
            parcel(layer, stage, i, False).start()
            parcel(layer, stage, i, True).start()

    def arrive(layer, stage):
        for i in partners(stage):
            parcel(layer, stage, i, False).wait_recv()
            parcel(layer, stage, i, True).wait_recv()
        total = taps_out[layer, stage]
        for i in partners(stage):
            total = total + taps_in[layer, stage, i - 1]
        taps_out[layer, stage + 1] = total

    def point_terms(layer):
        rows = up[layer].reshape(PARTS * CHAIN * ROWS, C)
        acts = active[layer].reshape(PARTS * CHAIN * ROWS, C)
        for m in range(2):
            part = rows[:, m * 384:(m + 1) * 384]
            for n in range(C // COLS):
                cols = slice(n * COLS, (n + 1) * COLS)
                product = lax.dot_general(
                    part, acts[:, cols], (((0,), (0,)), ((), ())), preferred_element_type=F32)
                product = product.astype(BF16).reshape(4, 2, 48, COLS)
                for owner in range(2):
                    terms[layer, owner, m * 4:(m + 1) * 4, :, cols] = product[:, owner]
        for t in range(3):
            line = jnp.sum(taps_acc[layer, t], axis=0, keepdims=True)
            for b in range(C // 128):
                taps_out[layer, 0, t, b:b + 1, :] = line[:, b * 128:(b + 1) * 128]

    def after_core(layer):
        @pl.loop(0, 8)
        def _(b):
            summed[layer, b // 4, b % 4] = (
                terms[layer, core, b].astype(F32) + sibling[layer, b].astype(F32)).astype(BF16)

    def after_x(layer):
        for b in range(C // 128):
            lanes = slice(b * 128, (b + 1) * 128)
            halves = []
            for half in range(2):
                total = summed[layer, half, x, :, lanes].astype(F32)
                for i in range(3):
                    total = total + from_x[layer, i, half, :, lanes].astype(F32)
                halves.append(total)
            halves.append(jnp.zeros((32, 128), F32))
            turned[lanes, :] = jnp.concatenate(halves, axis=0).T

        @pl.loop(0, 32)
        def _(g):
            value = turned[pl.ds(pl.multiple_of(g * 24, 8), 24), :]
            value = jnp.concatenate([value, jnp.zeros((8, 128), F32)], axis=0)
            to_y[layer, g // 8, g % 4, (g // 4) % 2] = value.astype(BF16)

    def after_y(layer):
        total = to_y[layer, y].astype(F32)
        for i in range(3):
            total = total + from_y[layer, i].astype(F32)
        to_z[layer] = total.astype(BF16)

    def after_z(layer):
        total = to_z[layer, c].astype(F32)
        for i in range(3):
            total = total + from_z[layer, i].astype(F32)
        to_block[layer] = total.astype(BF16)

    def after_block(layer):
        total = to_block[layer, h].astype(F32)
        for i in range(3):
            total = total + from_block[layer, i].astype(F32)
        upper = jnp.broadcast_to(zh, (24, 48)) > 0
        out_point[layer] = jnp.where(upper, total[0:24, 48:96], total[0:24, 0:48]) * factor
        sums = taps_out[layer, 5] * factor
        for t in range(3):
            for b in range(C // 128):
                out_taps[layer, t:t + 1, b * 128:(b + 1) * 128] = sums[t, b:b + 1, :]

    follow = (after_core, after_x, after_y, after_z, after_block)

    def advance(layer, stage):
        arrive(layer, stage)
        follow[stage](layer)
        if stage < 4:
            send(layer, stage + 1)

    def wait_dealt(src, slot, sends, recvs, own, a):
        @pl.loop(1, CHAIN)
        def _(i):
            dealt(src, slot, sends, recvs, a, i).wait_recv()

        own(a).wait()

    def send_back(a):
        @pl.loop(0, CHAIN - 1)
        def _(t):
            give_back(a, crossing_first(t)).start()

        own_out(a).start()

    for a in range(PARTS):
        wait_dealt(tok, tok_slot, tok_send, tok_recv, own_tok, a)
        forward(a)
    wait_dealt(cot, cot_slot, cot_send, cot_recv, own_cot, 0)
    for layer in (2, 1, 0):
        backward(0, layer)
    send_back(0)
    wait_dealt(cot, cot_slot, cot_send, cot_recv, own_cot, 1)
    backward(1, 2)
    point_terms(2)
    send(2, 0)
    backward(1, 1)
    point_terms(1)
    send(1, 0)
    advance(2, 0)
    backward(1, 0)
    send_back(1)
    point_terms(0)
    send(0, 0)
    advance(1, 0)
    advance(2, 1)
    advance(0, 0)
    advance(2, 2)
    advance(1, 1)
    advance(2, 3)
    advance(1, 2)
    advance(0, 1)
    advance(2, 4)
    advance(1, 3)
    advance(0, 2)
    advance(1, 4)
    advance(0, 3)
    advance(0, 4)

    for a in range(PARTS):
        own_out(a).wait()

        @pl.loop(1, CHAIN)
        def _(i):
            given_back(a, i).wait_recv()
            give_back(a, i).wait_send()
            deal(tok, tok_slot, tok_send, tok_recv, a, i).wait_send()
            deal(cot, cot_slot, cot_send, cot_recv, a, i).wait_send()
    for layer in range(LAYERS):
        for stage in range(5):
            for i in partners(stage):
                parcel(layer, stage, i, False).wait_send()
                parcel(layer, stage, i, True).wait_send()


def local(factor, tokens, cotangent, conv_kernel, point_weight):
    any_space = pl.BlockSpec(memory_space=pl.ANY)
    vmem = pl.BlockSpec(memory_space=pltpu.VMEM)
    part = (PARTS, CHAIN, ROWS, C)
    scratch = [
        pltpu.VMEM(part, BF16),
        pltpu.VMEM((LAYERS, PARTS, CHAIN + 8, ROWS, C), BF16),
        pltpu.VMEM((LAYERS,) + part, F32),
        pltpu.VMEM((LAYERS, PARTS, CHAIN, ROWS, 128), F32),
        pltpu.VMEM((LAYERS,) + part, F32),
        pltpu.VMEM((LAYERS,) + part, BF16),
        pltpu.VMEM((LAYERS,) + part, BF16),
        pltpu.VMEM((CHAIN, ROWS, C), F32),
        pltpu.VMEM((CHAIN + 8, ROWS, C), BF16),
        pltpu.VMEM(part, BF16),
        pltpu.VMEM((LAYERS, C, C), BF16),
        pltpu.VMEM((8, 128), F32),
        pltpu.VMEM((LAYERS, 2, 8, 48, C), BF16),
        pltpu.VMEM((LAYERS, 8, 48, C), BF16),
        pltpu.VMEM((LAYERS, 2, 4, 48, C), BF16),
        pltpu.VMEM((LAYERS, 3, 2, 48, C), BF16),
        pltpu.VMEM((C, 128), F32),
        pltpu.VMEM((LAYERS, 4, 4, 2, 32, 128), BF16),
        pltpu.VMEM((LAYERS, 3, 4, 2, 32, 128), BF16),
        pltpu.VMEM((LAYERS, 4, 2, 32, 128), BF16),
        pltpu.VMEM((LAYERS, 3, 2, 32, 128), BF16),
        pltpu.VMEM((LAYERS, 2, 32, 128), BF16),
        pltpu.VMEM((LAYERS, 3, 32, 128), BF16),
        pltpu.VMEM((LAYERS, 3, 8, C), F32),
        pltpu.VMEM((LAYERS, 6, 3, 8, 128), F32),
        pltpu.VMEM((LAYERS, 5, 3, 3, 8, 128), F32),
        pltpu.SemaphoreType.DMA((PARTS, CHAIN - 1)),
        pltpu.SemaphoreType.DMA((PARTS, CHAIN - 1)),
        pltpu.SemaphoreType.DMA((PARTS, CHAIN - 1)),
        pltpu.SemaphoreType.DMA((PARTS, CHAIN - 1)),
        pltpu.SemaphoreType.DMA((PARTS, CHAIN - 1)),
        pltpu.SemaphoreType.DMA((PARTS, CHAIN - 1)),
        pltpu.SemaphoreType.DMA((3 * PARTS,)),
        pltpu.SemaphoreType.DMA((LAYERS,)),
        pltpu.SemaphoreType.DMA((LAYERS, 5, 3, 2)),
        pltpu.SemaphoreType.DMA((LAYERS, 5, 3, 2)),
    ]
    out, out_point, out_taps = pl.pallas_call(
        functools.partial(kernel, factor),
        out_shape=(
            jax.ShapeDtypeStruct((SLAB, C), BF16),
            jax.ShapeDtypeStruct((LAYERS, 24, 48), F32),
            jax.ShapeDtypeStruct((LAYERS, 3, C), F32),
        ),
        in_specs=[any_space, any_space, vmem, any_space],
        out_specs=(any_space, vmem, vmem),
        scratch_shapes=scratch,
        compiler_params=pltpu.CompilerParams(collective_id=0, has_side_effects=True, vmem_limit_bytes=48 * 2**20),
        cost_estimate=pl.CostEstimate(flops=2 * 9 * SLAB * C * C, bytes_accessed=6 * 2**20, transcendentals=LAYERS * SLAB * C),
    )(tokens[0], cotangent[0], conv_kernel, point_weight)
    return out[None], out_point, out_taps


def solution(mesh):
    factor = 1.0 / math.sqrt(mesh.shape["seq"] * mesh.shape["dp"] * SLAB)
    P = jax.sharding.PartitionSpec
    return jax.shard_map(
        functools.partial(local, factor),
        mesh=mesh,
        in_specs=(P("dp", "seq", None), P("dp", "seq", None), P(), P()),
        out_specs=(P("dp", "seq", None), P(None, "seq", "dp"), P()),
        check_vma=False,
    )
```

time: 520 us -> 121 us (0.23)
  the two profiles are of different devices: /device:TPU:1 before, /device:TPU:64 now
where the time goes in v1:
time: 121 us
  Pallas kernels  113 us (93%)
  local copies, waits for them, and re-layouts  6.73 us (6%)
    pallas_call x1, Pallas kernels, local(): pl.pallas_call(functools.partial(kernel, factor), out_shape=(jax.ShapeDty...  113 us
    unnamed x11, local copies, waits for them, and re-layouts  6.73 us

profile of v1, /device:TPU:64, one launch (start us, length us, event | category | flops | bytes accessed | tf_op | source)
XLA Modules:
  0.0 120.8 jit_solution(3081248790302461028)
XLA Ops:
  0.6 0.0 copy-start
  0.6 2.0 %copy-done = bf16[3,768,768]{2,1,0:T(8,128)(2,1)S(1)} copy-done((bf16[3,768,768]{2,1,0:T(8,128)(2,1)S(1)}, bf16[3,768,768]{2,1,0:T(8,128)(2,1)}, u32[]{:S(2)}) %copy-start) | copy-done | bytes 3538968
  2.6 0.0 copy-start.1
  2.6 1.0 copy-done.1
  3.6 0.0 copy-start.2
  3.6 1.0 copy-done.2
  4.6 0.0 copy-start.3
  4.6 0.8 copy-done.3
  5.4 113.4 %shard_map.67 = (bf16[256,768]{1,0:T(8,128)(2,1)S(1)}, f32[3,24,48]{2,1,0:T(8,128)S(1)}, f32[3,3,768]{2,1,0:T(4,128)S(1)}) custom-call(bf16[256,768]{1,0:T(8,128)(2,1)S(1)} %bitcast.4, bf16[256,768]{1,0:T(8,128)(2,1)S(1)} %bitcast.5, f32[3,3,768]{2,1,0:T(4,128)S(1)} %copy-done.3, bf16[3,768,768]{2,1,0:T(8,128)(2,1)S(1)} %copy-done), custom_call_target="tpu_custom_call" | custom-call | flops 2717908992 | bytes 6291456 | tf_op jit(solution)/shard_map/pallas_call | solution.py:431
  118.8 0.7 copy.10
  119.6 0.6 copy.11
  120.2 0.6 copy.12
Async XLA Ops:
  0.6 2.0 %copy-start = (bf16[3,768,768]{2,1,0:T(8,128)(2,1)S(1)}, bf16[3,768,768]{2,1,0:T(8,128)(2,1)}, u32[]{:S(2)}) copy-start(bf16[3,768,768]{2,1,0:T(8,128)(2,1)} %weight.1) | copy-start | bytes 10616836
  2.6 1.0 copy-start.1
  3.6 1.0 copy-start.2
  4.6 0.8 copy-start.3

commit v2 on v1

v2 whole, which is shorter than its diff:
```python
import functools
import math

import jax
import jax.numpy as jnp
from jax import lax
from jax.experimental import pallas as pl
from jax.experimental.pallas import tpu as pltpu

EPSILON = 1e-06
MESH = pl.DeviceIdType.MESH
F32 = jnp.float32
BF16 = jnp.bfloat16

C = 768
LAYERS = 3
CHAIN = 8
ROWS = 16
PARTS = 2
SLAB = 256
COLS = 256
HALF = C // 2
PIECE = 96
GELU_A = math.sqrt(2.0 / math.pi)
GELU_B = 0.044715


def kernel(factor, tok, cot, taps_hbm, weight, out, out_point, out_taps, *scratch):
    (xin, normed, normal, inverse, slope, active, up, grad, grad_hid, ready, w, taps, terms, sibling, summed, half_way, from_a,
     turned, to_b, from_b, to_z, from_z, to_block, from_block, taps_acc, taps_part, taps_one, taps_in, taps_all,
     tok_send, tok_recv, cot_send, cot_recv, out_send, out_recv, own_sem, w_sem, core_sem, a_send, a_recv, red_send, red_recv,
     last_send, last_recv, tap_send, tap_recv) = scratch
    seq = lax.axis_index("seq")
    dp = lax.axis_index("dp")
    k, c = seq // 4, seq % 4
    y, h = seq // 8, (seq // 4) % 2
    zh, x, core = dp // 8, (dp // 2) % 4, dp % 2
    block = zh * 2 + h
    p = x + core * (y - x)
    r = y + core * (x - y)

    def chain_peer(i):
        j = (k + i) % CHAIN
        return j, (j * 4 + c, dp)

    def first_peer(place):
        return seq + core * (place - y) * 8, dp + (1 - core) * (place - x) * 2

    def step_peer(step, i):
        if step == 0:
            place = (r + i) % 4
            return place, (seq + (1 - core) * (place - y) * 8, dp + core * (place - x) * 2)
        place = (c + i) % 4
        return place, (seq - c + place, dp)

    def owner(e):
        return y * 8 + (e // 2) * 4 + c, core * 8 + x * 2 + e % 2

    def tap_peer(step, i):
        if step in (0, 4):
            place = (dp % 8 + i) % 8
            return place, (seq, zh * 8 + place)
        if step == 1:
            place = (y + i) % 4
            return place, (place * 8 + h * 4 + c, dp)
        if step == 2:
            return step_peer(1, i)
        place = (block + i) % 4
        return place, (y * 8 + (place % 2) * 4 + c, (place // 2) * 8 + dp % 8)

    barrier = pltpu.get_barrier_semaphore()

    def greet(peer):
        pl.semaphore_signal(barrier, inc=1, device_id=peer, device_id_type=MESH)

    @pl.loop(1, CHAIN)
    def _(i):
        greet(chain_peer(i)[1])
        greet(tap_peer(0, i)[1])

    @pl.loop(1, 4)
    def _(i):
        greet(step_peer(1, i)[1])

    @pl.loop(0, 4)
    def _(i):
        greet((y * 8 + (i // 2) * 4 + c, (1 - zh) * 8 + x * 2 + i % 2))

    greet((y * 8 + (1 - h) * 4 + c, zh * 8 + x * 2 + 1 - core))

    def load(layer):
        return pltpu.make_async_copy(weight.at[layer], w.at[layer], w_sem.at[layer])

    load_taps = pltpu.make_async_copy(taps_hbm, taps, w_sem.at[LAYERS])
    load_taps.start()
    for layer in range(LAYERS):
        load(layer).start()

    pl.semaphore_wait(barrier, 22)

    def rows_of(j, a):
        return pl.ds(pl.multiple_of(j * (PARTS * ROWS) + a * ROWS, ROWS), ROWS)

    def crossing_first(t):
        return 2 * t + 1 - 7 * (t // 4)

    def deal(src, dst_of, send, recv, a, i):
        j, peer = chain_peer(i)
        return pltpu.make_async_remote_copy(
            src_ref=src.at[rows_of(j, a)], dst_ref=dst_of(a, k), send_sem=send.at[a, i - 1], recv_sem=recv.at[a, i - 1],
            device_id=peer, device_id_type=MESH)

    def dealt(src, dst_of, send, recv, a, i):
        j = (k + CHAIN - i) % CHAIN
        return pltpu.make_async_remote_copy(
            src_ref=src.at[rows_of(j, a)], dst_ref=dst_of(a, j), send_sem=send.at[a, i - 1], recv_sem=recv.at[a, i - 1],
            device_id=chain_peer(i)[1], device_id_type=MESH)

    def tok_slot(a, j):
        return xin.at[a, j]

    def cot_slot(a, j):
        return up.at[LAYERS - 1, a, j]

    def own_tok(a):
        return pltpu.make_async_copy(tok.at[rows_of(k, a)], xin.at[a, k], own_sem.at[a])

    def own_cot(a):
        return pltpu.make_async_copy(cot.at[rows_of(k, a)], up.at[LAYERS - 1, a, k], own_sem.at[PARTS + a])

    def own_out(a):
        return pltpu.make_async_copy(ready.at[a, k], out.at[rows_of(k, a)], own_sem.at[2 * PARTS + a])

    def give_back(a, i):
        j, peer = chain_peer(i)
        return pltpu.make_async_remote_copy(
            src_ref=ready.at[a, j], dst_ref=out.at[rows_of(k, a)], send_sem=out_send.at[a, i - 1],
            recv_sem=out_recv.at[a, i - 1], device_id=peer, device_id_type=MESH)

    def given_back(a, i):
        j = (k + CHAIN - i) % CHAIN
        return pltpu.make_async_remote_copy(
            src_ref=ready.at[a, j], dst_ref=out.at[rows_of(j, a)], send_sem=out_send.at[a, i - 1],
            recv_sem=out_recv.at[a, i - 1], device_id=chain_peer(i)[1], device_id_type=MESH)

    for a in range(PARTS):
        @pl.loop(0, CHAIN - 1)
        def _(t):
            deal(tok, tok_slot, tok_send, tok_recv, a, crossing_first(t)).start()

        own_tok(a).start()
    for a in range(PARTS):
        @pl.loop(0, CHAIN - 1)
        def _(t):
            deal(cot, cot_slot, cot_send, cot_recv, a, crossing_first(t)).start()

        own_cot(a).start()
    zeros = jnp.zeros((4, ROWS, C), BF16)
    for layer in range(LAYERS):
        for a in range(PARTS):
            normed[layer, a, 0:4] = zeros
            normed[layer, a, 12:16] = zeros
    grad_hid[0:4] = zeros
    grad_hid[12:16] = zeros
    taps_acc[...] = jnp.zeros_like(taps_acc)
    taps_part[...] = jnp.zeros_like(taps_part)
    load_taps.wait()

    def forward(a):
        for layer in range(LAYERS):
            shift = 2**layer

            @pl.loop(0, CHAIN)
            def _(j):
                value = xin[a, j].astype(F32)
                mean = jnp.sum(value * value, axis=-1, keepdims=True) * (1.0 / C)
                inv = lax.rsqrt(mean + EPSILON)
                value = value * inv
                inverse[layer, a, j] = jnp.broadcast_to(inv, (ROWS, 128))
                normal[layer, a, j] = value
                normed[layer, a, 4 + j] = value.astype(BF16)

            @pl.loop(0, CHAIN)
            def _(j):
                hid = (
                    taps[layer, 0:1, :] * normed[layer, a, 4 + j - shift].astype(F32)
                    + taps[layer, 1:2, :] * normed[layer, a, 4 + j].astype(F32)
                    + taps[layer, 2:3, :] * normed[layer, a, 4 + j + shift].astype(F32)
                )
                square = hid * hid
                tanh = jnp.tanh(GELU_A * hid * (1.0 + GELU_B * square))
                half = 0.5 * (1.0 + tanh)
                active[layer, a, j] = (hid * half).astype(BF16)
                slope[layer, a, j] = half + (0.5 * GELU_A) * hid * (1.0 - tanh * tanh) * (1.0 + (3.0 * GELU_B) * square)

            if layer == LAYERS - 1:
                continue
            if a == 0:
                load(layer).wait()
            for n in range(C // COLS):
                cols = slice(n * COLS, (n + 1) * COLS)
                product = jnp.dot(active[layer, a].reshape(CHAIN * ROWS, C), w[layer, :, cols], preferred_element_type=F32)
                xin[a, :, :, cols] = (
                    xin[a, :, :, cols].astype(F32) + product.reshape(CHAIN, ROWS, COLS)).astype(BF16)

    def backward(a, layer):
        shift = 2**layer
        if a == 0 and layer == LAYERS - 1:
            load(layer).wait()
        for n in range(C // COLS):
            cols = slice(n * COLS, (n + 1) * COLS)
            spread = lax.dot_general(
                up[layer, a].reshape(CHAIN * ROWS, C), w[layer, cols, :], (((1,), (1,)), ((), ())),
                preferred_element_type=F32)
            grad_hid[4:12, :, cols] = (spread.reshape(CHAIN, ROWS, COLS) * slope[layer, a, :, :, cols]).astype(BF16)

        @pl.loop(0, CHAIN)
        def _(j):
            mid = grad_hid[4 + j].astype(F32)
            for t in range(3):
                term = mid * normed[layer, a, 4 + j + (t - 1) * shift].astype(F32)
                taps_acc[layer, t] += term[0:8] + term[8:16]
            moved = (
                taps[layer, 1:2, :] * mid
                + taps[layer, 0:1, :] * grad_hid[4 + j + shift].astype(F32)
                + taps[layer, 2:3, :] * grad_hid[4 + j - shift].astype(F32)
            )
            value = normal[layer, a, j]
            mean = jnp.sum(moved * value, axis=-1, keepdims=True) * (1.0 / C)
            before = up[layer, a, j].astype(F32) if layer == LAYERS - 1 else grad[j]
            after = before + inverse[layer, a, j, :, 0:1] * (moved - value * mean)
            if layer > 0:
                grad[j] = after
                up[layer - 1, a, j] = after.astype(BF16)
            else:
                ready[a, j] = after.astype(BF16)

    def point_terms(layer):
        rows = up[layer].reshape(PARTS * CHAIN * ROWS, C)
        acts = active[layer].reshape(PARTS * CHAIN * ROWS, C)
        over_rows = (((0,), (0,)), ((), ()))
        for m in range(2):
            some = acts[:, m * HALF:(m + 1) * HALF]
            product = lax.dot_general(rows[:, 0:HALF], some, over_rows, preferred_element_type=F32)
            terms[layer, 0, :, m] = product.astype(BF16).reshape(4, PIECE, HALF)
            product = lax.dot_general(some, rows[:, HALF:], over_rows, preferred_element_type=F32)
            terms[layer, 1, 2 * m:2 * m + 2] = product.astype(BF16).reshape(2, 2, PIECE, HALF)
        for t in range(3):
            line = jnp.sum(taps_acc[layer, t], axis=0, keepdims=True)
            for b in range(C // 128):
                row = (layer * 3 + t) * (C // 128) + b
                taps_part[row // 7, row % 7:row % 7 + 1, :] = line[:, b * 128:(b + 1) * 128]

    def to_sibling(layer):
        return pltpu.make_async_remote_copy(
            src_ref=terms.at[layer, 1 - core], dst_ref=sibling.at[layer], send_sem=core_sem.at[layer, 0],
            recv_sem=core_sem.at[layer, 1], device_id=(seq, dp + 1 - 2 * core), device_id_type=MESH)

    def around(layer, n):
        way = n % 2
        place = (p + 1 + 2 * way) % 4
        if n < 2:
            src, dst = summed.at[layer, (p + 2) % 4, way], half_way.at[layer, way]
        else:
            half = 1 - way if n < 4 else way
            src, dst = summed.at[layer, place, half], from_a.at[layer, way, half]
        return pltpu.make_async_remote_copy(
            src_ref=src, dst_ref=dst, send_sem=a_send.at[layer, n], recv_sem=a_recv.at[layer, n],
            device_id=first_peer(place), device_id_type=MESH)

    def parcel(layer, step, i):
        place, peer = step_peer(step, i)
        if step == 0:
            src, dst = to_b.at[layer, place], from_b.at[layer, i - 1]
        else:
            src, dst = to_z.at[layer, place], from_z.at[layer, i - 1]
        return pltpu.make_async_remote_copy(
            src_ref=src, dst_ref=dst, send_sem=red_send.at[layer, step, i - 1], recv_sem=red_recv.at[layer, step, i - 1],
            device_id=peer, device_id_type=MESH)

    def last_send_of(layer, e):
        return pltpu.make_async_remote_copy(
            src_ref=to_block.at[layer, e // 2], dst_ref=from_block.at[layer, block], send_sem=last_send.at[layer, e],
            recv_sem=last_recv.at[layer, block], device_id=owner(e), device_id_type=MESH)

    def last_arrival(layer, m):
        return pltpu.make_async_remote_copy(
            src_ref=to_block.at[layer, 0], dst_ref=from_block.at[layer, m], send_sem=last_send.at[layer, m],
            recv_sem=last_recv.at[layer, m], device_id=owner(m), device_id_type=MESH)

    def is_own(e):
        return jnp.logical_and(core == zh, e == h * 2 + core)

    def step_core(layer):
        to_sibling(layer).wait_recv()
        for q in (2, 1, 3, 0):
            place = (p + q) % 4
            summed[layer, place] = (
                terms[layer, core, place].astype(F32) + sibling[layer, place].astype(F32)).astype(BF16)
            if q == 2:
                around(layer, 0).start()
                around(layer, 1).start()
            if q == 1:
                around(layer, 2).start()
            if q == 3:
                around(layer, 3).start()

    def step_ring(layer):
        for way in range(2):
            around(layer, way).wait_recv()
            place = (p + 1 + 2 * way) % 4
            summed[layer, place, way] = (
                summed[layer, place, way].astype(F32) + half_way[layer, way].astype(F32)).astype(BF16)
            around(layer, 4 + way).start()

    def step_first(layer):
        for n in range(2, 6):
            around(layer, n).wait_recv()

        @pl.when(core == 0)
        def _():
            for half in range(2):
                for b in range(HALF // 128):
                    lanes = slice(b * 128, (b + 1) * 128)
                    total = (
                        summed[layer, p, half, :, lanes].astype(F32) + from_a[layer, 0, half, :, lanes].astype(F32)
                        + from_a[layer, 1, half, :, lanes].astype(F32))
                    total = jnp.concatenate([total, jnp.zeros((128 - PIECE, 128), F32)], axis=0)
                    turned[half * HALF + b * 128:half * HALF + (b + 1) * 128, :] = total.T

            @pl.loop(0, 32)
            def _(g):
                value = turned[pl.ds(pl.multiple_of(g * 24, 8), 24), :]
                value = jnp.concatenate([value, jnp.zeros((8, 128), F32)], axis=0)
                to_b[layer, g // 8, g % 4, (g // 4) % 2] = value.astype(BF16)

        @pl.when(core == 1)
        def _():
            for half in range(2):
                total = (
                    summed[layer, p, half].astype(F32) + from_a[layer, 0, half].astype(F32)
                    + from_a[layer, 1, half].astype(F32))
                for place in range(4):
                    value = total[:, place * PIECE:(place + 1) * PIECE]
                    value = jnp.concatenate([value, jnp.zeros((PIECE, 128 - PIECE), F32)], axis=1)
                    for g in range(4):
                        some = jnp.concatenate([value[g * 24:(g + 1) * 24], jnp.zeros((8, 128), F32)], axis=0)
                        to_b[layer, place, g, half] = some.astype(BF16)

        for i in range(1, 4):
            parcel(layer, 0, i).start()

    def step_second(layer):
        for i in range(1, 4):
            parcel(layer, 0, i).wait_recv()
        total = to_b[layer, r].astype(F32)
        for i in range(3):
            total = total + from_b[layer, i].astype(F32)
        to_z[layer] = total.astype(BF16)
        for i in range(1, 4):
            parcel(layer, 1, i).start()

    def step_z(layer):
        for i in range(1, 4):
            parcel(layer, 1, i).wait_recv()
        total = to_z[layer, c].astype(F32)
        for i in range(3):
            total = total + from_z[layer, i].astype(F32)
        to_block[layer] = total.astype(BF16)
        for e in range(4):
            @pl.when(is_own(e))
            def _():
                from_block[layer, block] = to_block[layer, e // 2]

            @pl.when(jnp.logical_not(is_own(e)))
            def _():
                last_send_of(layer, e).start()

    def step_last(layer):
        for m in range(4):
            @pl.when(jnp.logical_not(jnp.logical_and(core == zh, block == m)))
            def _():
                last_arrival(layer, m).wait_recv()
        total = from_block[layer, 0].astype(F32)
        for m in range(1, 4):
            total = total + from_block[layer, m].astype(F32)
        upper = jnp.broadcast_to(core, (24, 48)) > 0
        out_point[layer] = jnp.where(upper, total[0:24, 48:96], total[0:24, 0:48]) * factor

    def tap_partners(step):
        return range(1, 8 if step in (0, 4) else 4)

    def tap_copy(step, i):
        place, peer = tap_peer(step, i)
        if step == 0:
            src, dst = taps_part.at[place], taps_in.at[0, i - 1]
        elif step == 4:
            src, dst = taps_one.at[3], taps_all.at[dp % 8]
        else:
            src, dst = taps_one.at[step - 1], taps_in.at[step, i - 1]
        return pltpu.make_async_remote_copy(
            src_ref=src, dst_ref=dst, send_sem=tap_send.at[step, i - 1], recv_sem=tap_recv.at[step, i - 1],
            device_id=peer, device_id_type=MESH)

    def tap_gathered(i):
        place = (dp % 8 + 8 - i) % 8
        return pltpu.make_async_remote_copy(
            src_ref=taps_one.at[3], dst_ref=taps_all.at[place], send_sem=tap_send.at[4, i - 1],
            recv_sem=tap_recv.at[4, i - 1], device_id=tap_peer(4, i)[1], device_id_type=MESH)

    def tap_start(step):
        for i in tap_partners(step):
            tap_copy(step, i).start()

    def tap_step(step):
        for i in tap_partners(step):
            tap_copy(step, i).wait_recv()
        total = taps_part[dp % 8] if step == 0 else taps_one[step - 1]
        for i in tap_partners(step):
            total = total + taps_in[step, i - 1]
        taps_one[step] = total
        if step == 3:
            taps_all[dp % 8] = total
        tap_start(step + 1)

    def tap_last():
        for i in tap_partners(4):
            tap_gathered(i).wait_recv()
        for layer in range(LAYERS):
            for t in range(3):
                for b in range(C // 128):
                    row = (layer * 3 + t) * (C // 128) + b
                    out_taps[layer, t:t + 1, b * 128:(b + 1) * 128] = taps_all[row // 7, row % 7:row % 7 + 1, :] * factor

    def wait_dealt(src, slot, sends, recvs, own, a):
        @pl.loop(1, CHAIN)
        def _(i):
            dealt(src, slot, sends, recvs, a, i).wait_recv()

        own(a).wait()

    def send_back(a):
        @pl.loop(0, CHAIN - 1)
        def _(t):
            give_back(a, crossing_first(t)).start()

        own_out(a).start()

    for a in range(PARTS):
        wait_dealt(tok, tok_slot, tok_send, tok_recv, own_tok, a)
        forward(a)
    wait_dealt(cot, cot_slot, cot_send, cot_recv, own_cot, 0)
    for layer in (2, 1, 0):
        backward(0, layer)
    send_back(0)
    wait_dealt(cot, cot_slot, cot_send, cot_recv, own_cot, 1)
    backward(1, 2)
    point_terms(2)
    to_sibling(2).start()
    backward(1, 1)
    point_terms(1)
    to_sibling(1).start()
    step_core(2)
    backward(1, 0)
    send_back(1)
    point_terms(0)
    to_sibling(0).start()
    tap_start(0)
    step_core(1)
    step_ring(2)
    step_core(0)
    step_first(2)
    step_ring(1)
    tap_step(0)
    step_ring(0)
    step_first(1)
    step_second(2)
    tap_step(1)
    step_first(0)
    step_z(2)
    step_second(1)
    tap_step(2)
    step_second(0)
    step_z(1)
    step_last(2)
    tap_step(3)
    step_z(0)
    step_last(1)
    tap_last()
    step_last(0)

    for a in range(PARTS):
        own_out(a).wait()

        @pl.loop(1, CHAIN)
        def _(i):
            given_back(a, i).wait_recv()
            give_back(a, i).wait_send()
            deal(tok, tok_slot, tok_send, tok_recv, a, i).wait_send()
            deal(cot, cot_slot, cot_send, cot_recv, a, i).wait_send()
    for layer in range(LAYERS):
        to_sibling(layer).wait_send()
        for n in range(6):
            around(layer, n).wait_send()
        for step in range(2):
            for i in range(1, 4):
                parcel(layer, step, i).wait_send()
        for e in range(4):
            @pl.when(jnp.logical_not(is_own(e)))
            def _():
                last_send_of(layer, e).wait_send()
    for step in range(5):
        for i in tap_partners(step):
            tap_copy(step, i).wait_send()


def local(factor, tokens, cotangent, conv_kernel, point_weight):
    any_space = pl.BlockSpec(memory_space=pl.ANY)
    vmem = pl.BlockSpec(memory_space=pltpu.VMEM)
    part = (PARTS, CHAIN, ROWS, C)
    scratch = [
        pltpu.VMEM(part, BF16),
        pltpu.VMEM((LAYERS, PARTS, CHAIN + 8, ROWS, C), BF16),
        pltpu.VMEM((LAYERS,) + part, F32),
        pltpu.VMEM((LAYERS, PARTS, CHAIN, ROWS, 128), F32),
        pltpu.VMEM((LAYERS,) + part, F32),
        pltpu.VMEM((LAYERS,) + part, BF16),
        pltpu.VMEM((LAYERS,) + part, BF16),
        pltpu.VMEM((CHAIN, ROWS, C), F32),
        pltpu.VMEM((CHAIN + 8, ROWS, C), BF16),
        pltpu.VMEM(part, BF16),
        pltpu.VMEM((LAYERS, C, C), BF16),
        pltpu.VMEM((LAYERS, 3, C), F32),
        pltpu.VMEM((LAYERS, 2, 4, 2, PIECE, HALF), BF16),
        pltpu.VMEM((LAYERS, 4, 2, PIECE, HALF), BF16),
        pltpu.VMEM((LAYERS, 4, 2, PIECE, HALF), BF16),
        pltpu.VMEM((LAYERS, 2, PIECE, HALF), BF16),
        pltpu.VMEM((LAYERS, 2, 2, PIECE, HALF), BF16),
        pltpu.VMEM((C, 128), F32),
        pltpu.VMEM((LAYERS, 4, 4, 2, 32, 128), BF16),
        pltpu.VMEM((LAYERS, 3, 4, 2, 32, 128), BF16),
        pltpu.VMEM((LAYERS, 4, 2, 32, 128), BF16),
        pltpu.VMEM((LAYERS, 3, 2, 32, 128), BF16),
        pltpu.VMEM((LAYERS, 2, 32, 128), BF16),
        pltpu.VMEM((LAYERS, 4, 32, 128), BF16),
        pltpu.VMEM((LAYERS, 3, 8, C), F32),
        pltpu.VMEM((8, 8, 128), F32),
        pltpu.VMEM((4, 8, 128), F32),
        pltpu.VMEM((4, 7, 8, 128), F32),
        pltpu.VMEM((8, 8, 128), F32),
        pltpu.SemaphoreType.DMA((PARTS, CHAIN - 1)),
        pltpu.SemaphoreType.DMA((PARTS, CHAIN - 1)),
        pltpu.SemaphoreType.DMA((PARTS, CHAIN - 1)),
        pltpu.SemaphoreType.DMA((PARTS, CHAIN - 1)),
        pltpu.SemaphoreType.DMA((PARTS, CHAIN - 1)),
        pltpu.SemaphoreType.DMA((PARTS, CHAIN - 1)),
        pltpu.SemaphoreType.DMA((3 * PARTS,)),
        pltpu.SemaphoreType.DMA((LAYERS + 1,)),
        pltpu.SemaphoreType.DMA((LAYERS, 2)),
        pltpu.SemaphoreType.DMA((LAYERS, 6)),
        pltpu.SemaphoreType.DMA((LAYERS, 6)),
        pltpu.SemaphoreType.DMA((LAYERS, 2, 3)),
        pltpu.SemaphoreType.DMA((LAYERS, 2, 3)),
        pltpu.SemaphoreType.DMA((LAYERS, 4)),
        pltpu.SemaphoreType.DMA((LAYERS, 4)),
        pltpu.SemaphoreType.DMA((5, 7)),
        pltpu.SemaphoreType.DMA((5, 7)),
    ]
    out, out_point, out_taps = pl.pallas_call(
        functools.partial(kernel, factor),
        out_shape=(
            jax.ShapeDtypeStruct((SLAB, C), BF16),
            jax.ShapeDtypeStruct((LAYERS, 24, 48), F32),
            jax.ShapeDtypeStruct((LAYERS, 3, C), F32),
        ),
        in_specs=[any_space] * 4,
        out_specs=(any_space, vmem, vmem),
        scratch_shapes=scratch,
        compiler_params=pltpu.CompilerParams(collective_id=0, has_side_effects=True, vmem_limit_bytes=60 * 2**20),
        cost_estimate=pl.CostEstimate(flops=2 * 9 * SLAB * C * C, bytes_accessed=6 * 2**20, transcendentals=LAYERS * SLAB * C),
    )(tokens[0], cotangent[0], conv_kernel, point_weight)
    return out[None], out_point, out_taps


def solution(mesh):
    factor = 1.0 / math.sqrt(mesh.shape["seq"] * mesh.shape["dp"] * SLAB)
    P = jax.sharding.PartitionSpec
    return jax.shard_map(
        functools.partial(local, factor),
        mesh=mesh,
        in_specs=(P("dp", "seq", None), P("dp", "seq", None), P(), P()),
        out_specs=(P("dp", "seq", None), P(None, "seq", "dp"), P()),
        check_vma=False,
    )
```

time: 121 us -> 110 us (0.909)
  the two profiles are of different devices: /device:TPU:64 before, /device:TPU:1 now
where the time goes in v2:
time: 110 us
  Pallas kernels  104 us (95%)
  local copies, waits for them, and re-layouts  4.54 us (4%)
    pallas_call x1, Pallas kernels, local(): pl.pallas_call(functools.partial(kernel, factor), out_shape=(jax.ShapeDty...  104 us
    unnamed x3, local copies, waits for them, and re-layouts  4.54 us

profile of v2, /device:TPU:1, one launch (start us, length us, event | category | flops | bytes accessed | tf_op | source)
XLA Modules:
  0.0 109.6 jit_solution(5131721073142412746)
XLA Ops:
  0.6 104.4 %shard_map.67 = (bf16[256,768]{1,0:T(8,128)(2,1)}, f32[3,24,48]{2,1,0:T(8,128)}, f32[3,3,768]{2,1,0:T(4,128)}) custom-call(bf16[256,768]{1,0:T(8,128)(2,1)} %bitcast.4, bf16[256,768]{1,0:T(8,128)(2,1)} %bitcast.5, f32[3,3,768]{2,1,0:T(4,128)} %taps_hbm.1, bf16[3,768,768]{2,1,0:T(8,128)(2,1)} %weight.1), custom_call_target="tpu_custom_call" | custom-call | flops 2717908992 | bytes 6291456 | tf_op jit(solution)/shard_map/pallas_call | solution.py:569
  105.1 1.8 %copy.10 = bf16[1,256,768]{2,1,0:T(8,128)(2,1)} copy(bf16[1,256,768]{2,1,0:T(8,128)(2,1)} %bitcast.3) | data formatting | bytes 786432
  106.8 1.4 %copy.11 = f32[3,24,48]{2,1,0:T(8,128)} copy(f32[3,24,48]{2,1,0:T(8,128)} %get-tuple-element.13) | data formatting | bytes 27648
  108.2 1.4 %copy.12 = f32[3,3,768]{2,1,0:T(4,128)} copy(f32[3,3,768]{2,1,0:T(4,128)} %get-tuple-element.14) | data formatting | bytes 55296

commit v3 on v2

--- a/solution.py
+++ b/solution.py
@@ -27,9 +27,9 @@
 
 def kernel(factor, tok, cot, taps_hbm, weight, out, out_point, out_taps, *scratch):
     (xin, normed, normal, inverse, slope, active, up, grad, grad_hid, ready, w, taps, terms, sibling, summed, half_way, from_a,
-     turned, to_b, from_b, to_z, from_z, to_block, from_block, taps_acc, taps_part, taps_one, taps_in, taps_all,
+     turned, to_b, from_b, to_z, from_z, taps_acc, taps_part, taps_one, taps_in, taps_all,
      tok_send, tok_recv, cot_send, cot_recv, out_send, out_recv, own_sem, w_sem, core_sem, a_send, a_recv, red_send, red_recv,
-     last_send, last_recv, tap_send, tap_recv) = scratch
+     z_send, z_recv, tap_send, tap_recv, round_sem, pair_sem) = scratch
     seq = lax.axis_index("seq")
     dp = lax.axis_index("dp")
     k, c = seq // 4, seq % 4
@@ -46,27 +46,24 @@
     def first_peer(place):
         return seq + core * (place - y) * 8, dp + (1 - core) * (place - x) * 2
 
-    def step_peer(step, i):
-        if step == 0:
-            place = (r + i) % 4
-            return place, (seq + (1 - core) * (place - y) * 8, dp + core * (place - x) * 2)
-        place = (c + i) % 4
-        return place, (seq - c + place, dp)
-
-    def owner(e):
-        return y * 8 + (e // 2) * 4 + c, core * 8 + x * 2 + e % 2
+    def second_peer(i):
+        place = (r + i) % 4
+        return place, (seq + (1 - core) * (place - y) * 8, dp + core * (place - x) * 2)
+
+    z = zh * 8 + h * 4 + c
+
+    def z_device(place, of_core):
+        return y * 8 + place % 8, (place // 8) * 8 + x * 2 + of_core
 
     def tap_peer(step, i):
-        if step in (0, 4):
+        if step in (0, 3):
             place = (dp % 8 + i) % 8
             return place, (seq, zh * 8 + place)
         if step == 1:
             place = (y + i) % 4
             return place, (place * 8 + h * 4 + c, dp)
-        if step == 2:
-            return step_peer(1, i)
-        place = (block + i) % 4
-        return place, (y * 8 + (place % 2) * 4 + c, (place // 2) * 8 + dp % 8)
+        place = (z + i) % 16
+        return place, z_device(place, core)
 
     barrier = pltpu.get_barrier_semaphore()
 
@@ -78,15 +75,9 @@
         greet(chain_peer(i)[1])
         greet(tap_peer(0, i)[1])
 
-    @pl.loop(1, 4)
-    def _(i):
-        greet(step_peer(1, i)[1])
-
-    @pl.loop(0, 4)
-    def _(i):
-        greet((y * 8 + (i // 2) * 4 + c, (1 - zh) * 8 + x * 2 + i % 2))
-
-    greet((y * 8 + (1 - h) * 4 + c, zh * 8 + x * 2 + 1 - core))
+    above, below = z_device((z + 1) % 16, core), z_device((z + 15) % 16, core)
+    greet(above)
+    greet(below)
 
     def load(layer):
         return pltpu.make_async_copy(weight.at[layer], w.at[layer], w_sem.at[layer])
@@ -96,7 +87,7 @@
     for layer in range(LAYERS):
         load(layer).start()
 
-    pl.semaphore_wait(barrier, 22)
+    pl.semaphore_wait(barrier, 16)
 
     def rows_of(j, a):
         return pl.ds(pl.multiple_of(j * (PARTS * ROWS) + a * ROWS, ROWS), ROWS)
@@ -155,6 +146,16 @@
             deal(cot, cot_slot, cot_send, cot_recv, a, crossing_first(t)).start()
 
         own_cot(a).start()
+    @pl.loop(0, 8)
+    def _(t):
+        pl.semaphore_signal(round_sem.at[t, 0], inc=1, device_id=above, device_id_type=MESH)
+        pl.semaphore_signal(round_sem.at[t, 1], inc=1, device_id=below, device_id_type=MESH)
+        pl.semaphore_wait(round_sem.at[t, 0], 1)
+        pl.semaphore_wait(round_sem.at[t, 1], 1)
+
+    pl.semaphore_signal(pair_sem, inc=1, device_id=(seq, dp + 1 - 2 * core), device_id_type=MESH)
+    pl.semaphore_wait(pair_sem, 1)
+
     zeros = jnp.zeros((4, ROWS, C), BF16)
     for layer in range(LAYERS):
         for a in range(PARTS):
@@ -245,11 +246,14 @@
             terms[layer, 0, :, m] = product.astype(BF16).reshape(4, PIECE, HALF)
             product = lax.dot_general(some, rows[:, HALF:], over_rows, preferred_element_type=F32)
             terms[layer, 1, 2 * m:2 * m + 2] = product.astype(BF16).reshape(2, 2, PIECE, HALF)
-        for t in range(3):
-            line = jnp.sum(taps_acc[layer, t], axis=0, keepdims=True)
-            for b in range(C // 128):
-                row = (layer * 3 + t) * (C // 128) + b
-                taps_part[row // 7, row % 7:row % 7 + 1, :] = line[:, b * 128:(b + 1) * 128]
+
+    def tap_terms():
+        for layer in range(LAYERS):
+            for t in range(3):
+                line = jnp.sum(taps_acc[layer, t], axis=0, keepdims=True)
+                for b in range(C // 128):
+                    row = (layer * 3 + t) * (C // 128) + b
+                    taps_part[row // 7, row % 7:row % 7 + 1, :] = line[:, b * 128:(b + 1) * 128]
 
     def to_sibling(layer):
         return pltpu.make_async_remote_copy(
@@ -268,28 +272,25 @@
             src_ref=src, dst_ref=dst, send_sem=a_send.at[layer, n], recv_sem=a_recv.at[layer, n],
             device_id=first_peer(place), device_id_type=MESH)
 
-    def parcel(layer, step, i):
-        place, peer = step_peer(step, i)
-        if step == 0:
-            src, dst = to_b.at[layer, place], from_b.at[layer, i - 1]
-        else:
-            src, dst = to_z.at[layer, place], from_z.at[layer, i - 1]
-        return pltpu.make_async_remote_copy(
-            src_ref=src, dst_ref=dst, send_sem=red_send.at[layer, step, i - 1], recv_sem=red_recv.at[layer, step, i - 1],
-            device_id=peer, device_id_type=MESH)
-
-    def last_send_of(layer, e):
-        return pltpu.make_async_remote_copy(
-            src_ref=to_block.at[layer, e // 2], dst_ref=from_block.at[layer, block], send_sem=last_send.at[layer, e],
-            recv_sem=last_recv.at[layer, block], device_id=owner(e), device_id_type=MESH)
-
-    def last_arrival(layer, m):
-        return pltpu.make_async_remote_copy(
-            src_ref=to_block.at[layer, 0], dst_ref=from_block.at[layer, m], send_sem=last_send.at[layer, m],
-            recv_sem=last_recv.at[layer, m], device_id=owner(m), device_id_type=MESH)
+    def parcel(layer, i):
+        place, peer = second_peer(i)
+        return pltpu.make_async_remote_copy(
+            src_ref=to_b.at[layer, place], dst_ref=from_b.at[layer, i - 1], send_sem=red_send.at[layer, i - 1],
+            recv_sem=red_recv.at[layer, i - 1], device_id=peer, device_id_type=MESH)
+
+    def to_owner(e):
+        place = e // 2
+        return pltpu.make_async_remote_copy(
+            src_ref=to_z.at[e % 2, place], dst_ref=from_z.at[z], send_sem=z_send.at[e],
+            recv_sem=z_recv.at[z], device_id=z_device(core * 8 + place, e % 2), device_id_type=MESH)
+
+    def z_arrival(m):
+        return pltpu.make_async_remote_copy(
+            src_ref=to_z.at[0, 0], dst_ref=from_z.at[m], send_sem=z_send.at[m],
+            recv_sem=z_recv.at[m], device_id=z_device(m, zh), device_id_type=MESH)
 
     def is_own(e):
-        return jnp.logical_and(core == zh, e == h * 2 + core)
+        return jnp.logical_and(core == zh, e == (h * 4 + c) * 2 + core)
 
     def step_core(layer):
         to_sibling(layer).wait_recv()
@@ -332,7 +333,7 @@
             def _(g):
                 value = turned[pl.ds(pl.multiple_of(g * 24, 8), 24), :]
                 value = jnp.concatenate([value, jnp.zeros((8, 128), F32)], axis=0)
-                to_b[layer, g // 8, g % 4, (g // 4) % 2] = value.astype(BF16)
+                to_b[layer, g // 8, g % 8] = value.astype(BF16)
 
         @pl.when(core == 1)
         def _():
@@ -345,57 +346,64 @@
                     value = jnp.concatenate([value, jnp.zeros((PIECE, 128 - PIECE), F32)], axis=1)
                     for g in range(4):
                         some = jnp.concatenate([value[g * 24:(g + 1) * 24], jnp.zeros((8, 128), F32)], axis=0)
-                        to_b[layer, place, g, half] = some.astype(BF16)
+                        to_b[layer, place, half * 4 + g] = some.astype(BF16)
 
         for i in range(1, 4):
-            parcel(layer, 0, i).start()
-
-    def step_second(layer):
-        for i in range(1, 4):
-            parcel(layer, 0, i).wait_recv()
-        total = to_b[layer, r].astype(F32)
-        for i in range(3):
-            total = total + from_b[layer, i].astype(F32)
-        to_z[layer] = total.astype(BF16)
-        for i in range(1, 4):
-            parcel(layer, 1, i).start()
-
-    def step_z(layer):
-        for i in range(1, 4):
-            parcel(layer, 1, i).wait_recv()
-        total = to_z[layer, c].astype(F32)
-        for i in range(3):
-            total = total + from_z[layer, i].astype(F32)
-        to_block[layer] = total.astype(BF16)
-        for e in range(4):
+            parcel(layer, i).start()
+
+    def step_second():
+        totals = []
+        for layer in range(LAYERS):
+            for i in range(1, 4):
+                parcel(layer, i).wait_recv()
+            total = to_b[layer, r, :, 0:24].astype(F32)
+            for i in range(3):
+                total = total + from_b[layer, i, :, 0:24].astype(F32)
+            totals.append(total.reshape(8 * 24, 128))
+        for of_core in range(2):
+            first = of_core * 48
+            top = jnp.concatenate(
+                [totals[2][:, first:first + 48], totals[1][:, first:first + 48], totals[0][:, first:first + 32]], axis=1)
+            rest = totals[0][:, first + 32:first + 48].reshape(8, 3, 8, 16)
+            rest = [rest[:, g].reshape(64, 16) for g in range(3)] + [jnp.zeros((64, 80), F32)]
+            rest = jnp.concatenate(rest, axis=1)
+            whole = jnp.concatenate([top.reshape(8, 24, 128), rest.reshape(8, 8, 128)], axis=1)
+            to_z[of_core] = whole.astype(BF16)
+
+        @pl.loop(0, 16)
+        def _(e):
             @pl.when(is_own(e))
             def _():
-                from_block[layer, block] = to_block[layer, e // 2]
+                from_z[z] = to_z[core, h * 4 + c]
 
             @pl.when(jnp.logical_not(is_own(e)))
             def _():
-                last_send_of(layer, e).start()
-
-    def step_last(layer):
-        for m in range(4):
-            @pl.when(jnp.logical_not(jnp.logical_and(core == zh, block == m)))
+                to_owner(e).start()
+
+    def step_last():
+        @pl.loop(0, 16)
+        def _(m):
+            @pl.when(jnp.logical_not(jnp.logical_and(core == zh, z == m)))
             def _():
-                last_arrival(layer, m).wait_recv()
-        total = from_block[layer, 0].astype(F32)
-        for m in range(1, 4):
-            total = total + from_block[layer, m].astype(F32)
-        upper = jnp.broadcast_to(core, (24, 48)) > 0
-        out_point[layer] = jnp.where(upper, total[0:24, 48:96], total[0:24, 0:48]) * factor
-
-    def tap_partners(step):
-        return range(1, 8 if step in (0, 4) else 4)
+                z_arrival(m).wait_recv()
+
+        total = from_z[0].astype(F32)
+        for m in range(1, 16):
+            total = total + from_z[m].astype(F32)
+        total = total * factor
+        out_point[2] = total[0:24, 0:48]
+        out_point[1] = total[0:24, 48:96]
+        rest = jnp.concatenate([total[24:32, g * 16:(g + 1) * 16] for g in range(3)], axis=0)
+        out_point[0] = jnp.concatenate([total[0:24, 96:128], rest], axis=1)
+
+    tap_partners = (range(1, 8), range(1, 4), range(1, 16), range(1, 8))
 
     def tap_copy(step, i):
         place, peer = tap_peer(step, i)
         if step == 0:
             src, dst = taps_part.at[place], taps_in.at[0, i - 1]
-        elif step == 4:
-            src, dst = taps_one.at[3], taps_all.at[dp % 8]
+        elif step == 3:
+            src, dst = taps_one.at[2], taps_all.at[dp % 8]
         else:
             src, dst = taps_one.at[step - 1], taps_in.at[step, i - 1]
         return pltpu.make_async_remote_copy(
@@ -405,27 +413,32 @@
     def tap_gathered(i):
         place = (dp % 8 + 8 - i) % 8
         return pltpu.make_async_remote_copy(
-            src_ref=taps_one.at[3], dst_ref=taps_all.at[place], send_sem=tap_send.at[4, i - 1],
-            recv_sem=tap_recv.at[4, i - 1], device_id=tap_peer(4, i)[1], device_id_type=MESH)
+            src_ref=taps_one.at[2], dst_ref=taps_all.at[place], send_sem=tap_send.at[3, i - 1],
+            recv_sem=tap_recv.at[3, i - 1], device_id=tap_peer(3, i)[1], device_id_type=MESH)
 
     def tap_start(step):
-        for i in tap_partners(step):
+        @pl.loop(tap_partners[step].start, tap_partners[step].stop)
+        def _(i):
             tap_copy(step, i).start()
 
     def tap_step(step):
-        for i in tap_partners(step):
+        @pl.loop(tap_partners[step].start, tap_partners[step].stop)
+        def _(i):
             tap_copy(step, i).wait_recv()
+
         total = taps_part[dp % 8] if step == 0 else taps_one[step - 1]
-        for i in tap_partners(step):
+        for i in tap_partners[step]:
             total = total + taps_in[step, i - 1]
         taps_one[step] = total
-        if step == 3:
+        if step == 2:
             taps_all[dp % 8] = total
         tap_start(step + 1)
 
     def tap_last():
-        for i in tap_partners(4):
+        @pl.loop(1, 8)
+        def _(i):
             tap_gathered(i).wait_recv()
+
         for layer in range(LAYERS):
             for t in range(3):
                 for b in range(C // 128):
@@ -454,40 +467,33 @@
         backward(0, layer)
     send_back(0)
     wait_dealt(cot, cot_slot, cot_send, cot_recv, own_cot, 1)
-    backward(1, 2)
     point_terms(2)
     to_sibling(2).start()
-    backward(1, 1)
+    backward(1, 2)
     point_terms(1)
     to_sibling(1).start()
     step_core(2)
+    backward(1, 1)
+    point_terms(0)
+    to_sibling(0).start()
+    step_core(1)
+    step_ring(2)
     backward(1, 0)
     send_back(1)
-    point_terms(0)
-    to_sibling(0).start()
+    tap_terms()
     tap_start(0)
-    step_core(1)
-    step_ring(2)
     step_core(0)
+    step_ring(1)
     step_first(2)
-    step_ring(1)
+    step_ring(0)
     tap_step(0)
-    step_ring(0)
     step_first(1)
-    step_second(2)
+    step_first(0)
     tap_step(1)
-    step_first(0)
-    step_z(2)
-    step_second(1)
+    step_second()
     tap_step(2)
-    step_second(0)
-    step_z(1)
-    step_last(2)
-    tap_step(3)
-    step_z(0)
-    step_last(1)
+    step_last()
     tap_last()
-    step_last(0)
 
     for a in range(PARTS):
         own_out(a).wait()
@@ -502,15 +508,18 @@
         to_sibling(layer).wait_send()
         for n in range(6):
             around(layer, n).wait_send()
-        for step in range(2):
-            for i in range(1, 4):
-                parcel(layer, step, i).wait_send()
-        for e in range(4):
-            @pl.when(jnp.logical_not(is_own(e)))
-            def _():
-                last_send_of(layer, e).wait_send()
-    for step in range(5):
-        for i in tap_partners(step):
+        for i in range(1, 4):
+            parcel(layer, i).wait_send()
+
+    @pl.loop(0, 16)
+    def _(e):
+        @pl.when(jnp.logical_not(is_own(e)))
+        def _():
+            to_owner(e).wait_send()
+
+    for step in range(4):
+        @pl.loop(tap_partners[step].start, tap_partners[step].stop)
+        def _(i):
             tap_copy(step, i).wait_send()
 
 
@@ -537,16 +546,14 @@
         pltpu.VMEM((LAYERS, 2, PIECE, HALF), BF16),
         pltpu.VMEM((LAYERS, 2, 2, PIECE, HALF), BF16),
         pltpu.VMEM((C, 128), F32),
-        pltpu.VMEM((LAYERS, 4, 4, 2, 32, 128), BF16),
-        pltpu.VMEM((LAYERS, 3, 4, 2, 32, 128), BF16),
-        pltpu.VMEM((LAYERS, 4, 2, 32, 128), BF16),
-        pltpu.VMEM((LAYERS, 3, 2, 32, 128), BF16),
-        pltpu.VMEM((LAYERS, 2, 32, 128), BF16),
-        pltpu.VMEM((LAYERS, 4, 32, 128), BF16),
+        pltpu.VMEM((LAYERS, 4, 8, 32, 128), BF16),
+        pltpu.VMEM((LAYERS, 3, 8, 32, 128), BF16),
+        pltpu.VMEM((2, 8, 32, 128), BF16),
+        pltpu.VMEM((16, 32, 128), BF16),
         pltpu.VMEM((LAYERS, 3, 8, C), F32),
         pltpu.VMEM((8, 8, 128), F32),
-        pltpu.VMEM((4, 8, 128), F32),
-        pltpu.VMEM((4, 7, 8, 128), F32),
+        pltpu.VMEM((3, 8, 128), F32),
+        pltpu.VMEM((3, 15, 8, 128), F32),
         pltpu.VMEM((8, 8, 128), F32),
         pltpu.SemaphoreType.DMA((PARTS, CHAIN - 1)),
         pltpu.SemaphoreType.DMA((PARTS, CHAIN - 1)),
@@ -559,12 +566,14 @@
         pltpu.SemaphoreType.DMA((LAYERS, 2)),
         pltpu.SemaphoreType.DMA((LAYERS, 6)),
         pltpu.SemaphoreType.DMA((LAYERS, 6)),
-        pltpu.SemaphoreType.DMA((LAYERS, 2, 3)),
-        pltpu.SemaphoreType.DMA((LAYERS, 2, 3)),
-        pltpu.SemaphoreType.DMA((LAYERS, 4)),
-        pltpu.SemaphoreType.DMA((LAYERS, 4)),
-        pltpu.SemaphoreType.DMA((5, 7)),
-        pltpu.SemaphoreType.DMA((5, 7)),
+        pltpu.SemaphoreType.DMA((LAYERS, 3)),
+        pltpu.SemaphoreType.DMA((LAYERS, 3)),
+        pltpu.SemaphoreType.DMA((16,)),
+        pltpu.SemaphoreType.DMA((16,)),
+        pltpu.SemaphoreType.DMA((4, 15)),
+        pltpu.SemaphoreType.DMA((4, 15)),
+        pltpu.SemaphoreType.REGULAR((8, 2)),
+        pltpu.SemaphoreType.REGULAR,
     ]
     out, out_point, out_taps = pl.pallas_call(
         functools.partial(kernel, factor),

time: 110 us -> 103 us (0.936)
  Pallas kernels: 104 us -> 97.5 us
    pallas_call x1, Pallas kernels: 104 us -> 97.5 us  [local(): pl.pallas_call(functools.partial(kernel, factor), out_shape=(jax.ShapeDty...]
where the time goes in v3:
time: 103 us
  Pallas kernels  97.5 us (95%)
  local copies, waits for them, and re-layouts  4.54 us (4%)
    pallas_call x1, Pallas kernels, local(): pl.pallas_call(functools.partial(kernel, factor), out_shape=(jax.ShapeDty...  97.5 us
    unnamed x3, local copies, waits for them, and re-layouts  4.54 us

profile of v3, /device:TPU:1, one launch (start us, length us, event | category | flops | bytes accessed | tf_op | source)
XLA Modules:
  0.0 102.6 jit_solution(9307843270490737958)
XLA Ops:
  0.6 97.5 %shard_map.67 = (bf16[256,768]{1,0:T(8,128)(2,1)}, f32[3,24,48]{2,1,0:T(8,128)}, f32[3,3,768]{2,1,0:T(4,128)}) custom-call(bf16[256,768]{1,0:T(8,128)(2,1)} %bitcast.4, bf16[256,768]{1,0:T(8,128)(2,1)} %bitcast.5, f32[3,3,768]{2,1,0:T(4,128)} %taps_hbm.1, bf16[3,768,768]{2,1,0:T(8,128)(2,1)} %weight.1), custom_call_target="tpu_custom_call" | custom-call | flops 2717908992 | bytes 6291456 | tf_op jit(solution)/shard_map/pallas_call | solution.py:578
  98.1 1.8 %copy.10 = bf16[1,256,768]{2,1,0:T(8,128)(2,1)} copy(bf16[1,256,768]{2,1,0:T(8,128)(2,1)} %bitcast.3) | data formatting | bytes 786432
  99.9 1.4 %copy.11 = f32[3,24,48]{2,1,0:T(8,128)} copy(f32[3,24,48]{2,1,0:T(8,128)} %get-tuple-element.13) | data formatting | bytes 27648
  101.3 1.4 %copy.12 = f32[3,3,768]{2,1,0:T(4,128)} copy(f32[3,3,768]{2,1,0:T(4,128)} %get-tuple-element.14) | data formatting | bytes 55296

commit v4 on v3

--- a/solution.py
+++ b/solution.py
@@ -26,9 +26,9 @@
 
 
 def kernel(factor, tok, cot, taps_hbm, weight, out, out_point, out_taps, *scratch):
-    (xin, normed, normal, inverse, slope, active, up, grad, grad_hid, ready, w, taps, terms, sibling, summed, half_way, from_a,
-     turned, to_b, from_b, to_z, from_z, taps_acc, taps_part, taps_one, taps_in, taps_all,
-     tok_send, tok_recv, cot_send, cot_recv, out_send, out_recv, own_sem, w_sem, core_sem, a_send, a_recv, red_send, red_recv,
+    (xin, normed, normal, inverse, slope, active, up, grad, grad_hid, ready, w, taps, sib_active, sib_up, summed, half_way, from_a,
+     to_b, from_b, to_z, from_z, taps_acc, taps_part, taps_one, taps_in, taps_all,
+     tok_send, tok_recv, cot_send, cot_recv, out_send, out_recv, own_sem, w_sem, act_sem, up_sem, a_send, a_recv, red_send, red_recv,
      z_send, z_recv, tap_send, tap_recv, round_sem, pair_sem) = scratch
     seq = lax.axis_index("seq")
     dp = lax.axis_index("dp")
@@ -140,21 +140,54 @@
             deal(tok, tok_slot, tok_send, tok_recv, a, crossing_first(t)).start()
 
         own_tok(a).start()
-    for a in range(PARTS):
+    def send_cot(a):
+        for i in (1, 3, 5):
+            if a == 0:
+                deal(tok, tok_slot, tok_send, tok_recv, 0, i).wait_send()
+            else:
+                deal(cot, cot_slot, cot_send, cot_recv, 0, i).wait_send()
+
         @pl.loop(0, CHAIN - 1)
         def _(t):
             deal(cot, cot_slot, cot_send, cot_recv, a, crossing_first(t)).start()
 
         own_cot(a).start()
-    @pl.loop(0, 8)
-    def _(t):
+
+    def round_signal(t):
         pl.semaphore_signal(round_sem.at[t, 0], inc=1, device_id=above, device_id_type=MESH)
         pl.semaphore_signal(round_sem.at[t, 1], inc=1, device_id=below, device_id_type=MESH)
+
+    def round_wait(t):
         pl.semaphore_wait(round_sem.at[t, 0], 1)
         pl.semaphore_wait(round_sem.at[t, 1], 1)
 
-    pl.semaphore_signal(pair_sem, inc=1, device_id=(seq, dp + 1 - 2 * core), device_id_type=MESH)
-    pl.semaphore_wait(pair_sem, 1)
+    @pl.loop(0, 3)
+    def _(t):
+        round_signal(t)
+        round_wait(t)
+
+    round_signal(3)
+
+    def between_layers(n):
+        @pl.when(n < 5)
+        def _():
+            round_wait(3 + n)
+
+        @pl.when(n < 4)
+        def _():
+            round_signal(4 + n)
+
+        @pl.when(n == 3)
+        def _():
+            send_cot(1)
+
+        @pl.when(n == 4)
+        def _():
+            pl.semaphore_signal(pair_sem, inc=1, device_id=(seq, dp + 1 - 2 * core), device_id_type=MESH)
+
+        @pl.when(n == 5)
+        def _():
+            pl.semaphore_wait(pair_sem, 1)
 
     zeros = jnp.zeros((4, ROWS, C), BF16)
     for layer in range(LAYERS):
@@ -167,55 +200,83 @@
     taps_part[...] = jnp.zeros_like(taps_part)
     load_taps.wait()
 
-    def forward(a):
-        for layer in range(LAYERS):
-            shift = 2**layer
-
-            @pl.loop(0, CHAIN)
-            def _(j):
-                value = xin[a, j].astype(F32)
-                mean = jnp.sum(value * value, axis=-1, keepdims=True) * (1.0 / C)
-                inv = lax.rsqrt(mean + EPSILON)
-                value = value * inv
-                inverse[layer, a, j] = jnp.broadcast_to(inv, (ROWS, 128))
-                normal[layer, a, j] = value
-                normed[layer, a, 4 + j] = value.astype(BF16)
-
-            @pl.loop(0, CHAIN)
-            def _(j):
-                hid = (
-                    taps[layer, 0:1, :] * normed[layer, a, 4 + j - shift].astype(F32)
-                    + taps[layer, 1:2, :] * normed[layer, a, 4 + j].astype(F32)
-                    + taps[layer, 2:3, :] * normed[layer, a, 4 + j + shift].astype(F32)
-                )
-                square = hid * hid
-                tanh = jnp.tanh(GELU_A * hid * (1.0 + GELU_B * square))
-                half = 0.5 * (1.0 + tanh)
-                active[layer, a, j] = (hid * half).astype(BF16)
-                slope[layer, a, j] = half + (0.5 * GELU_A) * hid * (1.0 - tanh * tanh) * (1.0 + (3.0 * GELU_B) * square)
-
-            if layer == LAYERS - 1:
-                continue
-            if a == 0:
-                load(layer).wait()
-            for n in range(C // COLS):
-                cols = slice(n * COLS, (n + 1) * COLS)
+    pair = (seq, dp + 1 - 2 * core)
+
+    def give_active(layer, a):
+        return pltpu.make_async_remote_copy(
+            src_ref=active.at[layer, a], dst_ref=sib_active.at[layer, a], send_sem=act_sem.at[layer, a, 0],
+            recv_sem=act_sem.at[layer, a, 1], device_id=pair, device_id_type=MESH)
+
+    def give_up(layer, a):
+        return pltpu.make_async_remote_copy(
+            src_ref=up.at[layer, a, :, :, pl.ds(pl.multiple_of((1 - core) * HALF, HALF), HALF)],
+            dst_ref=sib_up.at[layer, a], send_sem=up_sem.at[layer, a, 0], recv_sem=up_sem.at[layer, a, 1],
+            device_id=pair, device_id_type=MESH)
+
+    def shift_of(layer):
+        return 1 + layer + layer * (layer - 1) // 2
+
+    def block_of_columns(n):
+        return pl.ds(pl.multiple_of(n * COLS, COLS), COLS)
+
+    def forward(a, layer):
+        shift = shift_of(layer)
+
+        @pl.loop(0, CHAIN, unroll=2)
+        def _(j):
+            value = xin[a, j].astype(F32)
+            mean = jnp.sum(value * value, axis=-1, keepdims=True) * (1.0 / C)
+            inv = lax.rsqrt(mean + EPSILON)
+            value = value * inv
+            inverse[layer, a, j] = jnp.broadcast_to(inv, (ROWS, 128))
+            normal[layer, a, j] = value
+            normed[layer, a, 4 + j] = value.astype(BF16)
+
+        @pl.loop(0, CHAIN, unroll=2)
+        def _(j):
+            hid = (
+                taps[layer, 0:1, :] * normed[layer, a, 4 + j - shift].astype(F32)
+                + taps[layer, 1:2, :] * normed[layer, a, 4 + j].astype(F32)
+                + taps[layer, 2:3, :] * normed[layer, a, 4 + j + shift].astype(F32)
+            )
+            square = hid * hid
+            tanh = jnp.tanh(GELU_A * hid * (1.0 + GELU_B * square))
+            half = 0.5 * (1.0 + tanh)
+            active[layer, a, j] = (hid * half).astype(BF16)
+            slope[layer, a, j] = half + (0.5 * GELU_A) * hid * (1.0 - tanh * tanh) * (1.0 + (3.0 * GELU_B) * square)
+
+        give_active(layer, a).start()
+        between_layers(a * LAYERS + layer)
+
+        @pl.when(a == 0)
+        def _():
+            load(layer).wait()
+
+        @pl.when(layer < LAYERS - 1)
+        def _():
+            @pl.loop(0, C // COLS)
+            def _(n):
+                cols = block_of_columns(n)
                 product = jnp.dot(active[layer, a].reshape(CHAIN * ROWS, C), w[layer, :, cols], preferred_element_type=F32)
                 xin[a, :, :, cols] = (
                     xin[a, :, :, cols].astype(F32) + product.reshape(CHAIN, ROWS, COLS)).astype(BF16)
 
     def backward(a, layer):
-        shift = 2**layer
-        if a == 0 and layer == LAYERS - 1:
-            load(layer).wait()
-        for n in range(C // COLS):
-            cols = slice(n * COLS, (n + 1) * COLS)
+        shift = shift_of(layer)
+
+        @pl.loop(0, C // COLS)
+        def _(n):
+            cols = block_of_columns(n)
             spread = lax.dot_general(
                 up[layer, a].reshape(CHAIN * ROWS, C), w[layer, cols, :], (((1,), (1,)), ((), ())),
                 preferred_element_type=F32)
             grad_hid[4:12, :, cols] = (spread.reshape(CHAIN, ROWS, COLS) * slope[layer, a, :, :, cols]).astype(BF16)
 
-        @pl.loop(0, CHAIN)
+        @pl.when(layer == LAYERS - 1)
+        def _():
+            grad[...] = up[layer, a].astype(F32)
+
+        @pl.loop(0, CHAIN, unroll=2)
         def _(j):
             mid = grad_hid[4 + j].astype(F32)
             for t in range(3):
@@ -228,24 +289,42 @@
             )
             value = normal[layer, a, j]
             mean = jnp.sum(moved * value, axis=-1, keepdims=True) * (1.0 / C)
-            before = up[layer, a, j].astype(F32) if layer == LAYERS - 1 else grad[j]
-            after = before + inverse[layer, a, j, :, 0:1] * (moved - value * mean)
-            if layer > 0:
-                grad[j] = after
+            after = grad[j] + inverse[layer, a, j, :, 0:1] * (moved - value * mean)
+            grad[j] = after
+            ready[a, j] = after.astype(BF16)
+
+            @pl.when(layer > 0)
+            def _():
                 up[layer - 1, a, j] = after.astype(BF16)
-            else:
-                ready[a, j] = after.astype(BF16)
 
     def point_terms(layer):
-        rows = up[layer].reshape(PARTS * CHAIN * ROWS, C)
-        acts = active[layer].reshape(PARTS * CHAIN * ROWS, C)
+        for a in range(PARTS):
+            give_active(layer, a).wait_recv()
+            give_up(layer, a).wait_recv()
+        mine = up[layer, :, :, :, pl.ds(pl.multiple_of(core * HALF, HALF), HALF)].reshape(SLAB, HALF)
+        rows = jnp.concatenate([mine, sib_up[layer].reshape(SLAB, HALF)], axis=0)
         over_rows = (((0,), (0,)), ((), ()))
-        for m in range(2):
-            some = acts[:, m * HALF:(m + 1) * HALF]
-            product = lax.dot_general(rows[:, 0:HALF], some, over_rows, preferred_element_type=F32)
-            terms[layer, 0, :, m] = product.astype(BF16).reshape(4, PIECE, HALF)
-            product = lax.dot_general(some, rows[:, HALF:], over_rows, preferred_element_type=F32)
-            terms[layer, 1, 2 * m:2 * m + 2] = product.astype(BF16).reshape(2, 2, PIECE, HALF)
+
+        def acts(m):
+            cols = slice(m * HALF, (m + 1) * HALF)
+            return jnp.concatenate(
+                [active[layer, :, :, :, cols].reshape(SLAB, HALF), sib_active[layer, :, :, :, cols].reshape(SLAB, HALF)],
+                axis=0)
+
+        @pl.when(core == 0)
+        def _():
+            for m in range(2):
+                product = lax.dot_general(rows, acts(m), over_rows, preferred_element_type=F32)
+                summed[layer, :, m] = product.astype(BF16).reshape(4, PIECE, HALF)
+
+        @pl.when(core == 1)
+        def _():
+            for m in range(2):
+                product = lax.dot_general(acts(m), rows, over_rows, preferred_element_type=F32)
+                summed[layer, 2 * m:2 * m + 2] = product.astype(BF16).reshape(2, 2, PIECE, HALF)
+
+        for n in range(4):
+            around(layer, n).start()
 
     def tap_terms():
         for layer in range(LAYERS):
@@ -254,11 +333,6 @@
                 for b in range(C // 128):
                     row = (layer * 3 + t) * (C // 128) + b
                     taps_part[row // 7, row % 7:row % 7 + 1, :] = line[:, b * 128:(b + 1) * 128]
-
-    def to_sibling(layer):
-        return pltpu.make_async_remote_copy(
-            src_ref=terms.at[layer, 1 - core], dst_ref=sibling.at[layer], send_sem=core_sem.at[layer, 0],
-            recv_sem=core_sem.at[layer, 1], device_id=(seq, dp + 1 - 2 * core), device_id_type=MESH)
 
     def around(layer, n):
         way = n % 2
@@ -292,20 +366,6 @@
     def is_own(e):
         return jnp.logical_and(core == zh, e == (h * 4 + c) * 2 + core)
 
-    def step_core(layer):
-        to_sibling(layer).wait_recv()
-        for q in (2, 1, 3, 0):
-            place = (p + q) % 4
-            summed[layer, place] = (
-                terms[layer, core, place].astype(F32) + sibling[layer, place].astype(F32)).astype(BF16)
-            if q == 2:
-                around(layer, 0).start()
-                around(layer, 1).start()
-            if q == 1:
-                around(layer, 2).start()
-            if q == 3:
-                around(layer, 3).start()
-
     def step_ring(layer):
         for way in range(2):
             around(layer, way).wait_recv()
@@ -327,13 +387,9 @@
                         summed[layer, p, half, :, lanes].astype(F32) + from_a[layer, 0, half, :, lanes].astype(F32)
                         + from_a[layer, 1, half, :, lanes].astype(F32))
                     total = jnp.concatenate([total, jnp.zeros((128 - PIECE, 128), F32)], axis=0)
-                    turned[half * HALF + b * 128:half * HALF + (b + 1) * 128, :] = total.T
-
-            @pl.loop(0, 32)
-            def _(g):
-                value = turned[pl.ds(pl.multiple_of(g * 24, 8), 24), :]
-                value = jnp.concatenate([value, jnp.zeros((8, 128), F32)], axis=0)
-                to_b[layer, g // 8, g % 8] = value.astype(BF16)
+                    first = half * HALF + b * 128
+                    for row in range(first, first + 128, 64):
+                        to_b[layer, row // 192, row % 192:row % 192 + 64, :] = total.T[row - first:row - first + 64].astype(BF16)
 
         @pl.when(core == 1)
         def _():
@@ -344,9 +400,7 @@
                 for place in range(4):
                     value = total[:, place * PIECE:(place + 1) * PIECE]
                     value = jnp.concatenate([value, jnp.zeros((PIECE, 128 - PIECE), F32)], axis=1)
-                    for g in range(4):
-                        some = jnp.concatenate([value[g * 24:(g + 1) * 24], jnp.zeros((8, 128), F32)], axis=0)
-                        to_b[layer, place, half * 4 + g] = some.astype(BF16)
+                    to_b[layer, place, half * PIECE:(half + 1) * PIECE, :] = value.astype(BF16)
 
         for i in range(1, 4):
             parcel(layer, i).start()
@@ -356,10 +410,10 @@
         for layer in range(LAYERS):
             for i in range(1, 4):
                 parcel(layer, i).wait_recv()
-            total = to_b[layer, r, :, 0:24].astype(F32)
+            total = to_b[layer, r].astype(F32)
             for i in range(3):
-                total = total + from_b[layer, i, :, 0:24].astype(F32)
-            totals.append(total.reshape(8 * 24, 128))
+                total = total + from_b[layer, i].astype(F32)
+            totals.append(total)
         for of_core in range(2):
             first = of_core * 48
             top = jnp.concatenate(
@@ -459,57 +513,96 @@
 
         own_out(a).start()
 
-    for a in range(PARTS):
-        wait_dealt(tok, tok_slot, tok_send, tok_recv, own_tok, a)
-        forward(a)
-    wait_dealt(cot, cot_slot, cot_send, cot_recv, own_cot, 0)
-    for layer in (2, 1, 0):
-        backward(0, layer)
-    send_back(0)
-    wait_dealt(cot, cot_slot, cot_send, cot_recv, own_cot, 1)
-    point_terms(2)
-    to_sibling(2).start()
-    backward(1, 2)
-    point_terms(1)
-    to_sibling(1).start()
-    step_core(2)
-    backward(1, 1)
-    point_terms(0)
-    to_sibling(0).start()
-    step_core(1)
-    step_ring(2)
-    backward(1, 0)
-    send_back(1)
+    send_cot(0)
+
+    @pl.loop(0, PARTS * LAYERS)
+    def _(n):
+        a, layer = n // LAYERS, n % LAYERS
+
+        @pl.when(layer == 0)
+        def _():
+            wait_dealt(tok, tok_slot, tok_send, tok_recv, own_tok, a)
+
+        forward(a, layer)
+
+    @pl.loop(0, PARTS * LAYERS)
+    def _(n):
+        a, layer = n // LAYERS, LAYERS - 1 - n % LAYERS
+
+        @pl.when(layer == LAYERS - 1)
+        def _():
+            wait_dealt(cot, cot_slot, cot_send, cot_recv, own_cot, a)
+            give_up(layer, a).start()
+
+        backward(a, layer)
+
+        @pl.when(layer > 0)
+        def _():
+            give_up(layer - 1, a).start()
+
+        @pl.when(layer == 0)
+        def _():
+            send_back(a)
+
+        @pl.when(a == PARTS - 1)
+        def _():
+            @pl.when(layer < LAYERS - 1)
+            def _():
+                step_ring(layer + 1)
+
+            point_terms(layer)
+
     tap_terms()
     tap_start(0)
-    step_core(0)
-    step_ring(1)
-    step_first(2)
-    step_ring(0)
-    tap_step(0)
-    step_first(1)
-    step_first(0)
-    tap_step(1)
+
+    @pl.loop(0, LAYERS)
+    def _(n):
+        @pl.when(n == 1)
+        def _():
+            step_ring(0)
+            tap_step(0)
+
+        @pl.when(n == 2)
+        def _():
+            tap_step(1)
+
+        step_first(LAYERS - 1 - n)
+
     step_second()
-    tap_step(2)
-    step_last()
-    tap_last()
 
     for a in range(PARTS):
         own_out(a).wait()
 
-        @pl.loop(1, CHAIN)
-        def _(i):
-            given_back(a, i).wait_recv()
+    @pl.loop(1, CHAIN)
+    def _(i):
+        for a in range(PARTS):
             give_back(a, i).wait_send()
-            deal(tok, tok_slot, tok_send, tok_recv, a, i).wait_send()
-            deal(cot, cot_slot, cot_send, cot_recv, a, i).wait_send()
-    for layer in range(LAYERS):
-        to_sibling(layer).wait_send()
+        deal(cot, cot_slot, cot_send, cot_recv, PARTS - 1, i).wait_send()
+
+    for i in range(1, CHAIN):
+        deal(tok, tok_slot, tok_send, tok_recv, 1, i).wait_send()
+    for i in (2, 4, 6, 7):
+        deal(tok, tok_slot, tok_send, tok_recv, 0, i).wait_send()
+        deal(cot, cot_slot, cot_send, cot_recv, 0, i).wait_send()
+    @pl.loop(0, LAYERS)
+    def _(layer):
+        for a in range(PARTS):
+            give_active(layer, a).wait_send()
+            give_up(layer, a).wait_send()
         for n in range(6):
             around(layer, n).wait_send()
         for i in range(1, 4):
             parcel(layer, i).wait_send()
+    for step in range(2):
+        @pl.loop(tap_partners[step].start, tap_partners[step].stop)
+        def _(i):
+            tap_copy(step, i).wait_send()
+
+    tap_step(2)
+    for a in range(PARTS):
+        @pl.loop(1, CHAIN)
+        def _(i):
+            given_back(a, i).wait_recv()
 
     @pl.loop(0, 16)
     def _(e):
@@ -517,10 +610,16 @@
         def _():
             to_owner(e).wait_send()
 
-    for step in range(4):
-        @pl.loop(tap_partners[step].start, tap_partners[step].stop)
-        def _(i):
-            tap_copy(step, i).wait_send()
+    @pl.loop(tap_partners[2].start, tap_partners[2].stop)
+    def _(i):
+        tap_copy(2, i).wait_send()
+
+    step_last()
+    tap_last()
+
+    @pl.loop(tap_partners[3].start, tap_partners[3].stop)
+    def _(i):
+        tap_copy(3, i).wait_send()
 
 
 def local(factor, tokens, cotangent, conv_kernel, point_weight):
@@ -540,14 +639,13 @@
         pltpu.VMEM(part, BF16),
         pltpu.VMEM((LAYERS, C, C), BF16),
         pltpu.VMEM((LAYERS, 3, C), F32),
-        pltpu.VMEM((LAYERS, 2, 4, 2, PIECE, HALF), BF16),
-        pltpu.VMEM((LAYERS, 4, 2, PIECE, HALF), BF16),
+        pltpu.VMEM((LAYERS,) + part, BF16),
+        pltpu.VMEM((LAYERS, PARTS, CHAIN, ROWS, HALF), BF16),
         pltpu.VMEM((LAYERS, 4, 2, PIECE, HALF), BF16),
         pltpu.VMEM((LAYERS, 2, PIECE, HALF), BF16),
         pltpu.VMEM((LAYERS, 2, 2, PIECE, HALF), BF16),
-        pltpu.VMEM((C, 128), F32),
-        pltpu.VMEM((LAYERS, 4, 8, 32, 128), BF16),
-        pltpu.VMEM((LAYERS, 3, 8, 32, 128), BF16),
+        pltpu.VMEM((LAYERS, 4, 192, 128), BF16),
+        pltpu.VMEM((LAYERS, 3, 192, 128), BF16),
         pltpu.VMEM((2, 8, 32, 128), BF16),
         pltpu.VMEM((16, 32, 128), BF16),
         pltpu.VMEM((LAYERS, 3, 8, C), F32),
@@ -563,7 +661,8 @@
         pltpu.SemaphoreType.DMA((PARTS, CHAIN - 1)),
         pltpu.SemaphoreType.DMA((3 * PARTS,)),
         pltpu.SemaphoreType.DMA((LAYERS + 1,)),
-        pltpu.SemaphoreType.DMA((LAYERS, 2)),
+        pltpu.SemaphoreType.DMA((LAYERS, PARTS, 2)),
+        pltpu.SemaphoreType.DMA((LAYERS, PARTS, 2)),
         pltpu.SemaphoreType.DMA((LAYERS, 6)),
         pltpu.SemaphoreType.DMA((LAYERS, 6)),
         pltpu.SemaphoreType.DMA((LAYERS, 3)),
@@ -578,9 +677,9 @@
     out, out_point, out_taps = pl.pallas_call(
         functools.partial(kernel, factor),
         out_shape=(
-            jax.ShapeDtypeStruct((SLAB, C), BF16),
-            jax.ShapeDtypeStruct((LAYERS, 24, 48), F32),
-            jax.ShapeDtypeStruct((LAYERS, 3, C), F32),
+            pltpu.VMEM((SLAB, C), BF16),
+            pltpu.VMEM((LAYERS, 24, 48), F32),
+            pltpu.VMEM((LAYERS, 3, C), F32),
         ),
         in_specs=[any_space] * 4,
         out_specs=(any_space, vmem, vmem),

time: 103 us -> 97.6 us (0.948)
  Pallas kernels: 97.5 us -> 94.9 us
  local copies, waits for them, and re-layouts: 4.54 us -> 1.98 us
    pallas_call x1, Pallas kernels: 97.5 us -> 94.9 us  [local(): pl.pallas_call(functools.partial(kernel, factor), out_shape=(pltpu.VMEM((...]
    unnamed x3, local copies, waits for them, and re-layouts: 4.54 us -> 1.98 us
where the time goes in v4:
time: 97.6 us; the launch traced here: 97.5 us
  Pallas kernels  94.9 us (97%)
  local copies, waits for them, and re-layouts  1.98 us (2%)
    pallas_call x1, Pallas kernels, local(): pl.pallas_call(functools.partial(kernel, factor), out_shape=(pltpu.VMEM((...  94.9 us
    unnamed x3, local copies, waits for them, and re-layouts  1.98 us

profile of v4, /device:TPU:1, one launch (start us, length us, event | category | flops | bytes accessed | tf_op | source)
XLA Modules:
  0.0 97.5 jit_solution(6202933089564039832)
XLA Ops:
  0.6 94.9 %shard_map.67 = (bf16[256,768]{1,0:T(8,128)(2,1)S(1)}, f32[3,24,48]{2,1,0:T(8,128)S(1)}, f32[3,3,768]{2,1,0:T(4,128)S(1)}) custom-call(bf16[256,768]{1,0:T(8,128)(2,1)} %bitcast.4, bf16[256,768]{1,0:T(8,128)(2,1)} %bitcast.5, f32[3,3,768]{2,1,0:T(4,128)} %taps_hbm.1, bf16[3,768,768]{2,1,0:T(8,128)(2,1)} %weight.1), custom_call_target="tpu_custom_call" | custom-call | flops 2717908992 | bytes 6291456 | tf_op jit(solution)/shard_map/pallas_call | solution.py:677
  95.5 0.7 copy.10
  96.3 0.6 copy.11
  96.9 0.6 copy.12

commit v5 on v4

--- a/solution.py
+++ b/solution.py
@@ -25,6 +25,14 @@
 GELU_B = 0.044715
 
 
+def div(a, b):
+    return lax.div(a, jnp.int32(b))
+
+
+def rem(a, b):
+    return lax.rem(a, jnp.int32(b))
+
+
 def kernel(factor, tok, cot, taps_hbm, weight, out, out_point, out_taps, *scratch):
     (xin, normed, normal, inverse, slope, active, up, grad, grad_hid, ready, w, taps, sib_active, sib_up, summed, half_way, from_a,
      to_b, from_b, to_z, from_z, taps_acc, taps_part, taps_one, taps_in, taps_all,
@@ -32,37 +40,40 @@
      z_send, z_recv, tap_send, tap_recv, round_sem, pair_sem) = scratch
     seq = lax.axis_index("seq")
     dp = lax.axis_index("dp")
-    k, c = seq // 4, seq % 4
-    y, h = seq // 8, (seq // 4) % 2
-    zh, x, core = dp // 8, (dp // 2) % 4, dp % 2
+    k, c = div(seq, 4), rem(seq, 4)
+    y, h = div(seq, 8), rem(k, 2)
+    zh, core = div(dp, 8), rem(dp, 2)
+    eighth = dp - zh * 8
+    x = div(eighth, 2)
     block = zh * 2 + h
     p = x + core * (y - x)
     r = y + core * (x - y)
 
     def chain_peer(i):
-        j = (k + i) % CHAIN
+        j = rem(k + i, CHAIN)
         return j, (j * 4 + c, dp)
 
     def first_peer(place):
         return seq + core * (place - y) * 8, dp + (1 - core) * (place - x) * 2
 
     def second_peer(i):
-        place = (r + i) % 4
+        place = rem(r + i, 4)
         return place, (seq + (1 - core) * (place - y) * 8, dp + core * (place - x) * 2)
 
     z = zh * 8 + h * 4 + c
 
     def z_device(place, of_core):
-        return y * 8 + place % 8, (place // 8) * 8 + x * 2 + of_core
+        half = div(place, 8)
+        return y * 8 + place - half * 8, half * 8 + x * 2 + of_core
 
     def tap_peer(step, i):
         if step in (0, 3):
-            place = (dp % 8 + i) % 8
+            place = rem(eighth + i, 8)
             return place, (seq, zh * 8 + place)
         if step == 1:
-            place = (y + i) % 4
+            place = rem(y + i, 4)
             return place, (place * 8 + h * 4 + c, dp)
-        place = (z + i) % 16
+        place = rem(z + i, 16)
         return place, z_device(place, core)
 
     barrier = pltpu.get_barrier_semaphore()
@@ -75,7 +86,7 @@
         greet(chain_peer(i)[1])
         greet(tap_peer(0, i)[1])
 
-    above, below = z_device((z + 1) % 16, core), z_device((z + 15) % 16, core)
+    above, below = z_device(rem(z + 1, 16), core), z_device(rem(z + 15, 16), core)
     greet(above)
     greet(below)
 
@@ -89,67 +100,62 @@
 
     pl.semaphore_wait(barrier, 16)
 
-    def rows_of(j, a):
-        return pl.ds(pl.multiple_of(j * (PARTS * ROWS) + a * ROWS, ROWS), ROWS)
-
     def crossing_first(t):
-        return 2 * t + 1 - 7 * (t // 4)
-
-    def deal(src, dst_of, send, recv, a, i):
+        return 2 * t + 1 - 7 * div(t, 4)
+
+    def deal_tok(a, i, arriving=False):
         j, peer = chain_peer(i)
-        return pltpu.make_async_remote_copy(
-            src_ref=src.at[rows_of(j, a)], dst_ref=dst_of(a, k), send_sem=send.at[a, i - 1], recv_sem=recv.at[a, i - 1],
-            device_id=peer, device_id_type=MESH)
-
-    def dealt(src, dst_of, send, recv, a, i):
-        j = (k + CHAIN - i) % CHAIN
-        return pltpu.make_async_remote_copy(
-            src_ref=src.at[rows_of(j, a)], dst_ref=dst_of(a, j), send_sem=send.at[a, i - 1], recv_sem=recv.at[a, i - 1],
-            device_id=chain_peer(i)[1], device_id_type=MESH)
-
-    def tok_slot(a, j):
-        return xin.at[a, j]
-
-    def cot_slot(a, j):
-        return up.at[LAYERS - 1, a, j]
+        slot = rem(k + CHAIN - i, CHAIN) if arriving else k
+        return pltpu.make_async_remote_copy(
+            src_ref=tok.at[j, a], dst_ref=xin.at[a, slot], send_sem=tok_send.at[a, i - 1],
+            recv_sem=tok_recv.at[a, i - 1], device_id=peer, device_id_type=MESH)
+
+    def deal_cot(a, i, arriving=False):
+        j, peer = chain_peer(i)
+        slot = rem(k + CHAIN - i, CHAIN) if arriving else k
+        return pltpu.make_async_remote_copy(
+            src_ref=cot.at[j, a], dst_ref=up.at[LAYERS - 1, a, slot], send_sem=cot_send.at[a, i - 1],
+            recv_sem=cot_recv.at[a, i - 1], device_id=peer, device_id_type=MESH)
 
     def own_tok(a):
-        return pltpu.make_async_copy(tok.at[rows_of(k, a)], xin.at[a, k], own_sem.at[a])
+        return pltpu.make_async_copy(tok.at[k, a], xin.at[a, k], own_sem.at[2 * PARTS + a])
 
     def own_cot(a):
-        return pltpu.make_async_copy(cot.at[rows_of(k, a)], up.at[LAYERS - 1, a, k], own_sem.at[PARTS + a])
+        return pltpu.make_async_copy(cot.at[k, a], up.at[LAYERS - 1, a, k], own_sem.at[PARTS + a])
 
     def own_out(a):
-        return pltpu.make_async_copy(ready.at[a, k], out.at[rows_of(k, a)], own_sem.at[2 * PARTS + a])
+        return pltpu.make_async_copy(ready.at[a, k], out.at[k, a], own_sem.at[a])
 
     def give_back(a, i):
         j, peer = chain_peer(i)
         return pltpu.make_async_remote_copy(
-            src_ref=ready.at[a, j], dst_ref=out.at[rows_of(k, a)], send_sem=out_send.at[a, i - 1],
+            src_ref=ready.at[a, j], dst_ref=out.at[k, a], send_sem=out_send.at[a, i - 1],
             recv_sem=out_recv.at[a, i - 1], device_id=peer, device_id_type=MESH)
 
     def given_back(a, i):
-        j = (k + CHAIN - i) % CHAIN
-        return pltpu.make_async_remote_copy(
-            src_ref=ready.at[a, j], dst_ref=out.at[rows_of(j, a)], send_sem=out_send.at[a, i - 1],
+        j = rem(k + CHAIN - i, CHAIN)
+        return pltpu.make_async_remote_copy(
+            src_ref=ready.at[a, j], dst_ref=out.at[j, a], send_sem=out_send.at[a, i - 1],
             recv_sem=out_recv.at[a, i - 1], device_id=chain_peer(i)[1], device_id_type=MESH)
 
-    for a in range(PARTS):
+    @pl.loop(0, PARTS)
+    def _(a):
         @pl.loop(0, CHAIN - 1)
         def _(t):
-            deal(tok, tok_slot, tok_send, tok_recv, a, crossing_first(t)).start()
+            deal_tok(a, crossing_first(t)).start()
 
         own_tok(a).start()
+
     def send_cot(a):
         for i in (1, 3, 5):
             if a == 0:
-                deal(tok, tok_slot, tok_send, tok_recv, 0, i).wait_send()
+                deal_tok(0, i).wait_send()
             else:
-                deal(cot, cot_slot, cot_send, cot_recv, 0, i).wait_send()
+                deal_cot(0, i).wait_send()
 
         @pl.loop(0, CHAIN - 1)
         def _(t):
-            deal(cot, cot_slot, cot_send, cot_recv, a, crossing_first(t)).start()
+            deal_cot(a, crossing_first(t)).start()
 
         own_cot(a).start()
 
@@ -214,7 +220,7 @@
             device_id=pair, device_id_type=MESH)
 
     def shift_of(layer):
-        return 1 + layer + layer * (layer - 1) // 2
+        return 1 + layer + div(layer * (layer - 1), 2)
 
     def block_of_columns(n):
         return pl.ds(pl.multiple_of(n * COLS, COLS), COLS)
@@ -222,7 +228,7 @@
     def forward(a, layer):
         shift = shift_of(layer)
 
-        @pl.loop(0, CHAIN, unroll=2)
+        @pl.loop(0, CHAIN, unroll=8)
         def _(j):
             value = xin[a, j].astype(F32)
             mean = jnp.sum(value * value, axis=-1, keepdims=True) * (1.0 / C)
@@ -232,7 +238,7 @@
             normal[layer, a, j] = value
             normed[layer, a, 4 + j] = value.astype(BF16)
 
-        @pl.loop(0, CHAIN, unroll=2)
+        @pl.loop(0, CHAIN, unroll=8)
         def _(j):
             hid = (
                 taps[layer, 0:1, :] * normed[layer, a, 4 + j - shift].astype(F32)
@@ -276,7 +282,7 @@
         def _():
             grad[...] = up[layer, a].astype(F32)
 
-        @pl.loop(0, CHAIN, unroll=2)
+        @pl.loop(0, CHAIN, unroll=8)
         def _(j):
             mid = grad_hid[4 + j].astype(F32)
             for t in range(3):
@@ -336,9 +342,9 @@
 
     def around(layer, n):
         way = n % 2
-        place = (p + 1 + 2 * way) % 4
+        place = rem(p + 1 + 2 * way, 4)
         if n < 2:
-            src, dst = summed.at[layer, (p + 2) % 4, way], half_way.at[layer, way]
+            src, dst = summed.at[layer, rem(p + 2, 4), way], half_way.at[layer, way]
         else:
             half = 1 - way if n < 4 else way
             src, dst = summed.at[layer, place, half], from_a.at[layer, way, half]
@@ -353,10 +359,11 @@
             recv_sem=red_recv.at[layer, i - 1], device_id=peer, device_id_type=MESH)
 
     def to_owner(e):
-        place = e // 2
-        return pltpu.make_async_remote_copy(
-            src_ref=to_z.at[e % 2, place], dst_ref=from_z.at[z], send_sem=z_send.at[e],
-            recv_sem=z_recv.at[z], device_id=z_device(core * 8 + place, e % 2), device_id_type=MESH)
+        place = div(e, 2)
+        of_core = e - place * 2
+        return pltpu.make_async_remote_copy(
+            src_ref=to_z.at[of_core, place], dst_ref=from_z.at[z], send_sem=z_send.at[e],
+            recv_sem=z_recv.at[z], device_id=z_device(core * 8 + place, of_core), device_id_type=MESH)
 
     def z_arrival(m):
         return pltpu.make_async_remote_copy(
@@ -369,7 +376,7 @@
     def step_ring(layer):
         for way in range(2):
             around(layer, way).wait_recv()
-            place = (p + 1 + 2 * way) % 4
+            place = rem(p + 1 + 2 * way, 4)
             summed[layer, place, way] = (
                 summed[layer, place, way].astype(F32) + half_way[layer, way].astype(F32)).astype(BF16)
             around(layer, 4 + way).start()
@@ -457,7 +464,7 @@
         if step == 0:
             src, dst = taps_part.at[place], taps_in.at[0, i - 1]
         elif step == 3:
-            src, dst = taps_one.at[2], taps_all.at[dp % 8]
+            src, dst = taps_one.at[2], taps_all.at[eighth]
         else:
             src, dst = taps_one.at[step - 1], taps_in.at[step, i - 1]
         return pltpu.make_async_remote_copy(
@@ -465,7 +472,7 @@
             device_id=peer, device_id_type=MESH)
 
     def tap_gathered(i):
-        place = (dp % 8 + 8 - i) % 8
+        place = rem(eighth + 8 - i, 8)
         return pltpu.make_async_remote_copy(
             src_ref=taps_one.at[2], dst_ref=taps_all.at[place], send_sem=tap_send.at[3, i - 1],
             recv_sem=tap_recv.at[3, i - 1], device_id=tap_peer(3, i)[1], device_id_type=MESH)
@@ -480,12 +487,12 @@
         def _(i):
             tap_copy(step, i).wait_recv()
 
-        total = taps_part[dp % 8] if step == 0 else taps_one[step - 1]
+        total = taps_part[eighth] if step == 0 else taps_one[step - 1]
         for i in tap_partners[step]:
             total = total + taps_in[step, i - 1]
         taps_one[step] = total
         if step == 2:
-            taps_all[dp % 8] = total
+            taps_all[eighth] = total
         tap_start(step + 1)
 
     def tap_last():
@@ -499,13 +506,6 @@
                     row = (layer * 3 + t) * (C // 128) + b
                     out_taps[layer, t:t + 1, b * 128:(b + 1) * 128] = taps_all[row // 7, row % 7:row % 7 + 1, :] * factor
 
-    def wait_dealt(src, slot, sends, recvs, own, a):
-        @pl.loop(1, CHAIN)
-        def _(i):
-            dealt(src, slot, sends, recvs, a, i).wait_recv()
-
-        own(a).wait()
-
     def send_back(a):
         @pl.loop(0, CHAIN - 1)
         def _(t):
@@ -517,21 +517,31 @@
 
     @pl.loop(0, PARTS * LAYERS)
     def _(n):
-        a, layer = n // LAYERS, n % LAYERS
+        a = div(n, LAYERS)
+        layer = n - a * LAYERS
 
         @pl.when(layer == 0)
         def _():
-            wait_dealt(tok, tok_slot, tok_send, tok_recv, own_tok, a)
+            @pl.loop(1, CHAIN)
+            def _(i):
+                deal_tok(a, i, arriving=True).wait_recv()
+
+            own_tok(a).wait()
 
         forward(a, layer)
 
     @pl.loop(0, PARTS * LAYERS)
     def _(n):
-        a, layer = n // LAYERS, LAYERS - 1 - n % LAYERS
+        a = div(n, LAYERS)
+        layer = LAYERS - 1 - (n - a * LAYERS)
 
         @pl.when(layer == LAYERS - 1)
         def _():
-            wait_dealt(cot, cot_slot, cot_send, cot_recv, own_cot, a)
+            @pl.loop(1, CHAIN)
+            def _(i):
+                deal_cot(a, i, arriving=True).wait_recv()
+
+            own_cot(a).wait()
             give_up(layer, a).start()
 
         backward(a, layer)
@@ -577,13 +587,13 @@
     def _(i):
         for a in range(PARTS):
             give_back(a, i).wait_send()
-        deal(cot, cot_slot, cot_send, cot_recv, PARTS - 1, i).wait_send()
-
-    for i in range(1, CHAIN):
-        deal(tok, tok_slot, tok_send, tok_recv, 1, i).wait_send()
+        deal_tok(PARTS - 1, i).wait_send()
+        deal_cot(PARTS - 1, i).wait_send()
+
     for i in (2, 4, 6, 7):
-        deal(tok, tok_slot, tok_send, tok_recv, 0, i).wait_send()
-        deal(cot, cot_slot, cot_send, cot_recv, 0, i).wait_send()
+        deal_tok(0, i).wait_send()
+        deal_cot(0, i).wait_send()
+
     @pl.loop(0, LAYERS)
     def _(layer):
         for a in range(PARTS):
@@ -626,6 +636,7 @@
     any_space = pl.BlockSpec(memory_space=pl.ANY)
     vmem = pl.BlockSpec(memory_space=pltpu.VMEM)
     part = (PARTS, CHAIN, ROWS, C)
+    dealt = (CHAIN, PARTS, ROWS, C)
     scratch = [
         pltpu.VMEM(part, BF16),
         pltpu.VMEM((LAYERS, PARTS, CHAIN + 8, ROWS, C), BF16),
@@ -677,7 +688,7 @@
     out, out_point, out_taps = pl.pallas_call(
         functools.partial(kernel, factor),
         out_shape=(
-            pltpu.VMEM((SLAB, C), BF16),
+            pltpu.VMEM((CHAIN, PARTS, ROWS, C), BF16),
             pltpu.VMEM((LAYERS, 24, 48), F32),
             pltpu.VMEM((LAYERS, 3, C), F32),
         ),
@@ -686,8 +697,8 @@
         scratch_shapes=scratch,
         compiler_params=pltpu.CompilerParams(collective_id=0, has_side_effects=True, vmem_limit_bytes=60 * 2**20),
         cost_estimate=pl.CostEstimate(flops=2 * 9 * SLAB * C * C, bytes_accessed=6 * 2**20, transcendentals=LAYERS * SLAB * C),
-    )(tokens[0], cotangent[0], conv_kernel, point_weight)
-    return out[None], out_point, out_taps
+    )(tokens.reshape(dealt), cotangent.reshape(dealt), conv_kernel, point_weight)
+    return out.reshape(tokens.shape), out_point, out_taps
 
 
 def solution(mesh):

time: 97.6 us -> 95.8 us (0.982)
  Pallas kernels: 94.9 us -> 93.1 us
    pallas_call x1, Pallas kernels: 94.9 us -> 93.1 us  [local(): pl.pallas_call(functools.partial(kernel, factor), out_shape=(pltpu.VMEM((...]
where the time goes in v5:
time: 95.8 us; the launch traced here: 95.7 us
  Pallas kernels  93.1 us (97%)
  local copies, waits for them, and re-layouts  1.98 us (2%)
    pallas_call x1, Pallas kernels, local(): pl.pallas_call(functools.partial(kernel, factor), out_shape=(pltpu.VMEM((...  93.1 us
    unnamed x3, local copies, waits for them, and re-layouts  1.98 us

profile of v5, /device:TPU:1, one launch (start us, length us, event | category | flops | bytes accessed | tf_op | source)
XLA Modules:
  0.0 95.7 jit_solution(7984218158327110616)
XLA Ops:
  0.6 93.1 %shard_map.67 = (bf16[8,2,16,768]{3,2,1,0:T(8,128)(2,1)S(1)}, f32[3,24,48]{2,1,0:T(8,128)S(1)}, f32[3,3,768]{2,1,0:T(4,128)S(1)}) custom-call(bf16[8,2,16,768]{3,2,1,0:T(8,128)(2,1)} %bitcast.4, bf16[8,2,16,768]{3,2,1,0:T(8,128)(2,1)} %bitcast.5, f32[3,3,768]{2,1,0:T(4,128)} %taps_hbm.1, bf16[3,768,768]{2,1,0:T(8,128)(2,1)} %weight.1), custom_call_target="tpu_custom_call" | custom-call | flops 2717908992 | bytes 6291456 | tf_op jit(solution)/shard_map/pallas_call | solution.py:688
  93.7 0.7 copy.10
  94.5 0.6 copy.11
  95.1 0.6 copy.12

commit v6 on v5

--- a/solution.py
+++ b/solution.py
@@ -34,7 +34,7 @@
 
 
 def kernel(factor, tok, cot, taps_hbm, weight, out, out_point, out_taps, *scratch):
-    (xin, normed, normal, inverse, slope, active, up, grad, grad_hid, ready, w, taps, sib_active, sib_up, summed, half_way, from_a,
+    (xin, normed, normal, inverse, slope, active, up, grad, grad_hid, w, taps, sib_active, sib_up, summed, half_way, from_a,
      to_b, from_b, to_z, from_z, taps_acc, taps_part, taps_one, taps_in, taps_all,
      tok_send, tok_recv, cot_send, cot_recv, out_send, out_recv, own_sem, w_sem, act_sem, up_sem, a_send, a_recv, red_send, red_recv,
      z_send, z_recv, tap_send, tap_recv, round_sem, pair_sem) = scratch
@@ -114,28 +114,28 @@
         j, peer = chain_peer(i)
         slot = rem(k + CHAIN - i, CHAIN) if arriving else k
         return pltpu.make_async_remote_copy(
-            src_ref=cot.at[j, a], dst_ref=up.at[LAYERS - 1, a, slot], send_sem=cot_send.at[a, i - 1],
+            src_ref=cot.at[j, a], dst_ref=up.at[LAYERS, a, slot], send_sem=cot_send.at[a, i - 1],
             recv_sem=cot_recv.at[a, i - 1], device_id=peer, device_id_type=MESH)
 
     def own_tok(a):
         return pltpu.make_async_copy(tok.at[k, a], xin.at[a, k], own_sem.at[2 * PARTS + a])
 
     def own_cot(a):
-        return pltpu.make_async_copy(cot.at[k, a], up.at[LAYERS - 1, a, k], own_sem.at[PARTS + a])
+        return pltpu.make_async_copy(cot.at[k, a], up.at[LAYERS, a, k], own_sem.at[PARTS + a])
 
     def own_out(a):
-        return pltpu.make_async_copy(ready.at[a, k], out.at[k, a], own_sem.at[a])
+        return pltpu.make_async_copy(up.at[0, a, k], out.at[k, a], own_sem.at[a])
 
     def give_back(a, i):
         j, peer = chain_peer(i)
         return pltpu.make_async_remote_copy(
-            src_ref=ready.at[a, j], dst_ref=out.at[k, a], send_sem=out_send.at[a, i - 1],
+            src_ref=up.at[0, a, j], dst_ref=out.at[k, a], send_sem=out_send.at[a, i - 1],
             recv_sem=out_recv.at[a, i - 1], device_id=peer, device_id_type=MESH)
 
     def given_back(a, i):
         j = rem(k + CHAIN - i, CHAIN)
         return pltpu.make_async_remote_copy(
-            src_ref=ready.at[a, j], dst_ref=out.at[j, a], send_sem=out_send.at[a, i - 1],
+            src_ref=up.at[0, a, j], dst_ref=out.at[j, a], send_sem=out_send.at[a, i - 1],
             recv_sem=out_recv.at[a, i - 1], device_id=chain_peer(i)[1], device_id_type=MESH)
 
     @pl.loop(0, PARTS)
@@ -215,7 +215,7 @@
 
     def give_up(layer, a):
         return pltpu.make_async_remote_copy(
-            src_ref=up.at[layer, a, :, :, pl.ds(pl.multiple_of((1 - core) * HALF, HALF), HALF)],
+            src_ref=up.at[layer + 1, a, :, :, pl.ds(pl.multiple_of((1 - core) * HALF, HALF), HALF)],
             dst_ref=sib_up.at[layer, a], send_sem=up_sem.at[layer, a, 0], recv_sem=up_sem.at[layer, a, 1],
             device_id=pair, device_id_type=MESH)
 
@@ -274,13 +274,13 @@
         def _(n):
             cols = block_of_columns(n)
             spread = lax.dot_general(
-                up[layer, a].reshape(CHAIN * ROWS, C), w[layer, cols, :], (((1,), (1,)), ((), ())),
+                up[layer + 1, a].reshape(CHAIN * ROWS, C), w[layer, cols, :], (((1,), (1,)), ((), ())),
                 preferred_element_type=F32)
             grad_hid[4:12, :, cols] = (spread.reshape(CHAIN, ROWS, COLS) * slope[layer, a, :, :, cols]).astype(BF16)
 
         @pl.when(layer == LAYERS - 1)
         def _():
-            grad[...] = up[layer, a].astype(F32)
+            grad[...] = up[layer + 1, a].astype(F32)
 
         @pl.loop(0, CHAIN, unroll=8)
         def _(j):
@@ -297,17 +297,13 @@
             mean = jnp.sum(moved * value, axis=-1, keepdims=True) * (1.0 / C)
             after = grad[j] + inverse[layer, a, j, :, 0:1] * (moved - value * mean)
             grad[j] = after
-            ready[a, j] = after.astype(BF16)
-
-            @pl.when(layer > 0)
-            def _():
-                up[layer - 1, a, j] = after.astype(BF16)
+            up[layer, a, j] = after.astype(BF16)
 
     def point_terms(layer):
         for a in range(PARTS):
             give_active(layer, a).wait_recv()
             give_up(layer, a).wait_recv()
-        mine = up[layer, :, :, :, pl.ds(pl.multiple_of(core * HALF, HALF), HALF)].reshape(SLAB, HALF)
+        mine = up[layer + 1, :, :, :, pl.ds(pl.multiple_of(core * HALF, HALF), HALF)].reshape(SLAB, HALF)
         rows = jnp.concatenate([mine, sib_up[layer].reshape(SLAB, HALF)], axis=0)
         over_rows = (((0,), (0,)), ((), ()))
 
@@ -644,10 +640,9 @@
         pltpu.VMEM((LAYERS, PARTS, CHAIN, ROWS, 128), F32),
         pltpu.VMEM((LAYERS,) + part, F32),
         pltpu.VMEM((LAYERS,) + part, BF16),
-        pltpu.VMEM((LAYERS,) + part, BF16),
+        pltpu.VMEM((LAYERS + 1,) + part, BF16),
         pltpu.VMEM((CHAIN, ROWS, C), F32),
         pltpu.VMEM((CHAIN + 8, ROWS, C), BF16),
-        pltpu.VMEM(part, BF16),
         pltpu.VMEM((LAYERS, C, C), BF16),
         pltpu.VMEM((LAYERS, 3, C), F32),
         pltpu.VMEM((LAYERS,) + part, BF16),

time: 95.8 us -> 100 us (1.044)
  Pallas kernels: 93.1 us -> 97.2 us
    pallas_call x1, Pallas kernels: 93.1 us -> 97.2 us  [local(): pl.pallas_call(functools.partial(kernel, factor), out_shape=(pltpu.VMEM((...]
where the time goes in v6:
time: 100 us; the launch traced here: 99.9 us
  Pallas kernels  97.2 us (97%)
  local copies, waits for them, and re-layouts  1.98 us (2%)
    pallas_call x1, Pallas kernels, local(): pl.pallas_call(functools.partial(kernel, factor), out_shape=(pltpu.VMEM((...  97.2 us

profile of v6, /device:TPU:1, one launch (start us, length us, event | category | flops | bytes accessed | tf_op | source)
XLA Modules:
  0.0 99.9 jit_solution(16352575025049476504)
XLA Ops:
  0.6 97.2 %shard_map.67 = (bf16[8,2,16,768]{3,2,1,0:T(8,128)(2,1)S(1)}, f32[3,24,48]{2,1,0:T(8,128)S(1)}, f32[3,3,768]{2,1,0:T(4,128)S(1)}) custom-call(bf16[8,2,16,768]{3,2,1,0:T(8,128)(2,1)} %bitcast.4, bf16[8,2,16,768]{3,2,1,0:T(8,128)(2,1)} %bitcast.5, f32[3,3,768]{2,1,0:T(4,128)} %taps_hbm.1, bf16[3,768,768]{2,1,0:T(8,128)(2,1)} %weight.1), custom_call_target="tpu_custom_call" | custom-call | flops 2717908992 | bytes 6291456 | tf_op jit(solution)/shard_map/pallas_call | solution.py:683
  97.9 0.7 copy.10
  98.6 0.6 copy.11
  99.2 0.6 copy.12
